TPU v7x, 32 devices: a whole 2x2x4 slice. The times are simulated.
32 devices in a mesh: cam: 4 (over x, core), tile: 8 (over z, y).
Axes of the slice: x: 2, y: 2, z: 4, core: 2. Of those that a mesh axis runs over, the one named last changes fastest.
Arguments:
- depth_weights: bfloat16 [128, 16, 64, 128], P(('cam', 'tile')), may hold values from 0.049804688 to 1
- context: bfloat16 [128, 16, 128, 128], P(('cam', 'tile')), may hold values from -1.5 to 1.5
- block_owner: int32 [128, 16, 1], P(('cam', 'tile')), may hold values from 0 to 31; in each aligned block of 64 rows (0 to 63, 64 to 127, ..., all dimensions but the last counted through in order) at most 4 rows name the same one
- block_local: int32 [128, 16], P(('cam', 'tile')), may hold values from 0 to 15
- block_cell: int32 [128, 16, 64], P(('cam', 'tile')), may hold values from 0 to 255
- conv_weight: bfloat16 [4, 3, 3, 128, 128], replicated, may hold values from -0.25 to 0.25
- cotangent: bfloat16 [64, 2048, 128], P('cam', 'tile'), may hold values from -6 to 6
Outputs:
- bev_out: bfloat16 [64, 2048, 128], P('cam', 'tile')
- grad_depth: bfloat16 [128, 16, 64, 128], P(('cam', 'tile'))
- grad_context: bfloat16 [128, 16, 128, 128], P(('cam', 'tile'))
Inputs may be any that keep to these rules, and one draw needn't show every extreme that they name: `block_owner`: among the blocks of the cameras of one device (aligned groups of 4 cameras) no owner is named by more than 4 blocks, a bound that some block reaches.
All inputs are finite; a program needn't handle non-finite values.
Results may differ from a plain program's by a relative error of at most 0.02.
Values may be sent and summed in bfloat16 or wider, within the bound.
A program may use at most 128 MiB of HBM per device.

v0:
```python
import jax
import jax.numpy as jnp
from jax import lax
from jax.sharding import PartitionSpec as P

TS = 16
LAYERS = 4


def extended(cells, sides, width):
    for axis, dim in sides:
        count = lax.axis_size(axis)
        ends = count - 1
        head = lax.slice_in_dim(cells, 0, width, axis=dim)
        tail = lax.slice_in_dim(cells, cells.shape[dim] - width, cells.shape[dim], axis=dim)
        cells = jnp.concatenate(
            [
                lax.ppermute(tail, axis, [(i, (i + 1) % count) for i in range(ends)]),
                cells,
                lax.ppermute(head, axis, [((i + 1) % count, i) for i in range(ends)]),
            ],
            axis=dim,
        )
    return cells


def silu_slope(preact):
    sigma = jax.nn.sigmoid(preact)
    return sigma * (1.0 + preact * (1.0 - sigma))


def conv_taps(padded, kernel, flipped):
    rows_out = padded.shape[0] - 2
    cols_out = padded.shape[1] - 2
    total = jnp.zeros((rows_out, cols_out, kernel.shape[3]), jnp.float32)
    for row_tap in range(3):
        for col_tap in range(3):
            window = padded[row_tap : row_tap + rows_out, col_tap : col_tap + cols_out]
            if flipped:
                total = total + jnp.einsum(
                    "xyo,io->xyi",
                    window,
                    kernel[2 - row_tap, 2 - col_tap],
                    preferred_element_type=jnp.float32,
                )
            else:
                total = total + jnp.einsum(
                    "xyi,io->xyo",
                    window,
                    kernel[row_tap, col_tap],
                    preferred_element_type=jnp.float32,
                )
    return total


def per_device(
    depth_weights, context, block_owner, block_local, block_cell, conv_weight, cotangent
):
    cams_here, blocks_cam, bins, pixels = depth_weights.shape
    channels = context.shape[3]
    rows_here = cotangent.shape[0]
    cols_here = cotangent.shape[1]
    cam_devices = lax.axis_size("cam")
    tile_devices = lax.axis_size("tile")
    owner_count = cam_devices * tile_devices
    blocks_here = cams_here * blocks_cam
    capacity = max(2, 2 * blocks_here // owner_count)
    slots_total = owner_count * capacity
    flat_depth = depth_weights.reshape(blocks_here, bins, pixels)
    flat_context = context.reshape(blocks_here, pixels, channels)
    lifted = jnp.einsum(
        "bdp,bpc->bdc", flat_depth, flat_context, preferred_element_type=jnp.float32
    ).astype(jnp.bfloat16)
    owner_ids = block_owner.reshape(blocks_here)
    positions = jnp.arange(blocks_here, dtype=jnp.int32)
    earlier_same = (owner_ids[:, None] == owner_ids[None, :]) & (
        positions[None, :] < positions[:, None]
    )
    rank_within = jnp.sum(earlier_same.astype(jnp.int32), axis=1)
    slot_index = owner_ids * capacity + rank_within
    tiles_across = cols_here // TS
    tiles_down = rows_here // TS
    tile_count = tiles_across * tiles_down
    tile_cells = TS * TS
    local_ids = block_local.reshape(blocks_here)
    cell_ids = block_cell.reshape(blocks_here, bins)
    row_start = local_ids // tiles_across * TS
    col_start = local_ids % tiles_across * TS
    region_cell = (
        (row_start[:, None] + cell_ids // TS) * cols_here + col_start[:, None] + cell_ids % TS
    )
    send_rows = jnp.zeros((slots_total, bins, channels), jnp.bfloat16).at[slot_index].set(lifted)
    send_cells = jnp.zeros((slots_total, bins), jnp.int32).at[slot_index].set(region_cell)
    recv_rows, recv_cells = (
        lax.all_to_all(send_rows, ("cam", "tile"), split_axis=0, concat_axis=0, tiled=True),
        lax.all_to_all(send_cells, ("cam", "tile"), split_axis=0, concat_axis=0, tiled=True),
    )
    cell_row = recv_cells // cols_here
    cell_col = recv_cells % cols_here
    within_tile = cell_row % TS * TS + cell_col % TS
    slot_tile = cell_row[:, 0] // TS * tiles_across + cell_col[:, 0] // TS
    cell_onehot = (
        jnp.arange(tile_cells, dtype=jnp.int32)[None, :, None] == within_tile[:, None, :]
    ).astype(jnp.bfloat16)
    tile_onehot = jnp.arange(tile_count, dtype=jnp.int32)[:, None] == slot_tile[None, :]
    slot_sums = jnp.einsum(
        "sed,sdc->sec", cell_onehot, recv_rows, preferred_element_type=jnp.float32
    )
    tile_sums = jnp.einsum(
        "ts,sec->tec", tile_onehot.astype(jnp.float32), slot_sums, precision=lax.Precision.HIGHEST
    )
    tile_grid = tile_sums.reshape(tiles_down, tiles_across, TS, TS, channels).transpose(
        0, 2, 1, 3, 4
    )
    activation = tile_grid.reshape(rows_here, cols_here, channels).astype(jnp.bfloat16)
    stored = []
    current = extended(activation, (("cam", 0), ("tile", 1)), LAYERS)
    row_first = lax.axis_index("cam") * rows_here
    col_first = lax.axis_index("tile") * cols_here
    for layer in range(LAYERS):
        preact = conv_taps(current, conv_weight[layer], False)
        margin = LAYERS - layer - 1
        row_global = row_first - margin + jnp.arange(rows_here + 2 * margin, dtype=jnp.int32)
        col_global = col_first - margin + jnp.arange(cols_here + 2 * margin, dtype=jnp.int32)
        row_inside = (row_global >= 0) & (row_global < rows_here * cam_devices)
        col_inside = (col_global >= 0) & (col_global < cols_here * tile_devices)
        inside = (row_inside[:, None] & col_inside[None, :]).astype(jnp.float32)
        current = (jax.nn.silu(preact) * inside[:, :, None]).astype(jnp.bfloat16)
        stored.append(preact[margin : margin + rows_here, margin : margin + cols_here])
    activation = current
    gradient = cotangent
    for layer in range(LAYERS - 1, -1, -1):
        grad_pre = (gradient.astype(jnp.float32) * silu_slope(stored[layer])).astype(jnp.bfloat16)
        padded_grad = extended(grad_pre, (("cam", 0), ("tile", 1)), 1)
        gradient = conv_taps(padded_grad, conv_weight[layer], True).astype(jnp.bfloat16)
    grad_tiles = (
        gradient.reshape(tiles_down, TS, tiles_across, TS, channels)
        .transpose(0, 2, 1, 3, 4)
        .reshape(tile_count, tile_cells, channels)
    )
    slot_grad = jnp.einsum(
        "ts,tec->sec",
        tile_onehot.astype(jnp.bfloat16),
        grad_tiles,
        preferred_element_type=jnp.float32,
    ).astype(jnp.bfloat16)
    grad_rows = jnp.einsum(
        "sed,sec->sdc", cell_onehot, slot_grad, preferred_element_type=jnp.float32
    ).astype(jnp.bfloat16)
    returned = lax.all_to_all(grad_rows, ("cam", "tile"), split_axis=0, concat_axis=0, tiled=True)
    block_grad = returned[slot_index]
    grad_context = jnp.einsum(
        "bdp,bdc->bpc", flat_depth, block_grad, preferred_element_type=jnp.float32
    ).astype(jnp.bfloat16)
    grad_depth = jnp.einsum(
        "bdc,bpc->bdp", block_grad, flat_context, preferred_element_type=jnp.float32
    ).astype(jnp.bfloat16)
    return (
        activation,
        grad_depth.reshape(depth_weights.shape),
        grad_context.reshape(context.shape),
    )


def solution(mesh):
    placed = (
        P(("cam", "tile"), None, None, None),
        P(("cam", "tile"), None, None, None),
        P(("cam", "tile"), None, None),
        P(("cam", "tile"), None),
        P(("cam", "tile"), None, None),
        P(),
        P("cam", "tile", None),
    )
    return jax.shard_map(
        per_device,
        mesh=mesh,
        in_specs=placed,
        out_specs=(
            P("cam", "tile", None),
            P(("cam", "tile"), None, None, None),
            P(("cam", "tile"), None, None, None),
        ),
        check_vma=False,
    )
```

profile of v0, /device:TPU:0, one launch (start us, length us, event | category | flops | bytes accessed | tf_op | source)
XLA Modules:
  0.0 346.4 jit_solution(16955258160916937333)
XLA Ops:
  6.9 7.3 %all-to-all-start = ((s32[32,1,256]{2,1,0:T(1,128)}), s32[32,1,256]{2,1,0:T(1,128)S(1)}, u32[]{:S(2)}, u32[]{:S(2)}) async-start(s32[32,1,256]{2,1,0:T(1,128)} %reshape.505), calls=%async_computation | async-start | bytes 65536 | tf_op jit(solution)/shard_map/all_to_all | solution.py:96
  18.0 8.1 %scatter_fusion = bf16[128,64,128]{2,1,0:T(8,128)(2,1)} fusion(bf16[128,64,128]{2,1,0:T(8,128)(2,1)} %broadcast_in_dim.5, s32[64]{0:T(128)S(1)} %fusion.222, bf16[64,64,128]{2,1,0:T(8,128)(2,1)S(1)} %convolution_convert_fusion.3), kind=kCustom, calls=%fused_computation.2 | custom fusion | bytes 3145984 | tf_op jit(solution)/shard_map/scatter | solution.py:92
  26.2 6.0 %all-to-all-start.1 = ((bf16[128,64,128]{2,1,0:T(8,128)(2,1)}), bf16[128,64,128]{2,1,0:T(8,128)(2,1)}, u32[]{:S(2)}, u32[]{:S(2)}) async-start(bf16[128,64,128]{2,1,0:T(8,128)(2,1)} %scatter_fusion), calls=%async_computation.1 | async-start | bytes 4194304 | tf_op jit(solution)/shard_map/all_to_all | solution.py:95
  34.1 48.1 %all-to-all-done.1 = bf16[128,64,128]{2,1,0:T(8,128)(2,1)} async-done(((bf16[128,64,128]{2,1,0:T(8,128)(2,1)}), bf16[128,64,128]{2,1,0:T(8,128)(2,1)}, u32[]{:S(2)}, u32[]{:S(2)}) %all-to-all-start.1) | async-done | bytes 2097184 | tf_op jit(solution)/shard_map/all_to_all | solution.py:95
  82.2 8.6 %fusion.4 = f32[128,256,128]{2,1,0:T(8,128)S(1)} fusion(bf16[128,64,128]{2,1,0:T(8,128)(2,1)} %all-to-all-done.1, s32[128,64]{1,0:T(8,128)S(1)} %get-tuple-element.52), kind=kOutput, calls=%fused_computation.8 | convolution fusion | flops 538968064 | bytes 18907136 | tf_op jit(solution)/shard_map/sed,sdc->sec/dot_general | solution.py:106
  90.8 15.1 %fusion.10 = bf16[16,256,128]{2,0,1:T(8,128)(2,1)S(1)} fusion(f32[128,256,128]{2,1,0:T(8,128)S(1)} %fusion.4, s32[128]{0:T(128)S(1)} %fusion.223), kind=kOutput, calls=%fused_computation.32 | convolution fusion | flops 805832704 | bytes 17826304 | tf_op jit(solution)/shard_map/ts,sec->tec/dot_general | solution.py:109
  107.6 3.0 collective-permute-start
  113.1 4.5 %collective-permute-start.2 = (bf16[24,4,128]{2,1,0:T(4,128)(2,1)S(1)}, bf16[24,4,128]{2,1,0:T(4,128)(2,1)S(1)}, u32[]{:S(2)}, u32[]{:S(2)}) collective-permute-start(bf16[24,4,128]{2,1,0:T(4,128)(2,1)S(1)} %get-tuple-element.19), channel_id=1, source_target_pairs={{0,1},{1,2},{2,3},{3,4},{4,5},{5,6},{6,7},{8,9},{9,10},{10,11},{11... | collective-permute-start | bytes 73736 | tf_op jit(solution)/shard_map/ppermute | solution.py:18
  125.4 2.6 fusion.31
  128.0 2.5 fusion.29
  130.5 6.5 %multiply_convert_fusion = (bf16[22,262,128]{2,1,0:T(8,128)(2,1)S(1)}, f32[22,262,128]{2,1,0:T(8,128)}) fusion(f32[22,262]{1,0:T(8,128)S(1)} %and_convert_fusion.2, bf16[3,3,128,128]{3,2,1,0:T(8,128)(2,1)} %copy-done.4, bf16[24,264,128]{2,1,0:T(8,128)(2,1)S(1)} %pad_maximum_fusion, f32[22,262,128]{2,1,0:T(8,128)S(1)} %fusion.17, ...), kind=kOutput, calls=%fused_computation.12 | convolution fusion | flops 199203840 | bytes 29772800 | tf_op jit(solution)/shard_map/xyi,io->xyo/dot_general | solution.py:47
  143.0 2.4 fusion.46
  145.4 5.3 %multiply_convert_fusion.1 = (bf16[20,260,128]{2,1,0:T(8,128)(2,1)S(1)}, f32[20,260,128]{2,1,0:T(8,128)}) fusion(f32[20,260]{1,0:T(8,128)S(1)} %and_convert_fusion.1, bf16[3,3,128,128]{3,2,1,0:T(8,128)(2,1)S(1)} %get-tuple-element.38, bf16[22,262,128]{2,1,0:T(8,128)(2,1)S(1)} %get-tuple-element.58, f32[20,260,128]{2,1,0:T(8,128)S(1)} %fusion.34, ...), kind=kOutput, calls=%fused_computation.14 | convolution fusion | flops 179712000 | bytes 27000832 | tf_op jit(solution)/shard_map/xyi,io->xyo/dot_general | solution.py:47
  163.1 2.7 multiply_convert_fusion.6
  167.1 4.4 %collective-permute-start.4 = (bf16[1,256,128]{2,1,0:T(8,128)(2,1)S(1)}, bf16[1,256,128]{2,1,0:T(8,128)(2,1)S(1)}, u32[]{:S(2)}, u32[]{:S(2)}) collective-permute-start(bf16[1,256,128]{2,1,0:T(8,128)(2,1)S(1)} %get-tuple-element.47), channel_id=1, source_target_pairs={{0,8},{8,16},{16,24},{1,9},{9,17},{17,25},{2,10},{10,18},{18,26},{... | collective-permute-start | bytes 196616 | tf_op jit(solution)/shard_map/ppermute | solution.py:18
  173.8 5.0 %collective-permute-start.6 = (bf16[18,1,128]{2,1,0:T(2,128)(2,1)S(1)}, bf16[18,1,128]{2,1,0:T(2,128)(2,1)S(1)}, u32[]{:S(2)}, u32[]{:S(2)}) collective-permute-start(bf16[18,1,128]{2,1,0:T(2,128)(2,1)S(1)} %get-tuple-element.36), channel_id=1, source_target_pairs={{0,1},{1,2},{2,3},{3,4},{4,5},{5,6},{6,7},{8,9},{9,10},{10,11},{11... | collective-permute-start | bytes 13832 | tf_op jit(solution)/shard_map/ppermute | solution.py:18
  182.6 1.9 multiply_convert_fusion.5
  185.8 6.5 %collective-permute-start.8 = (bf16[1,256,128]{2,1,0:T(8,128)(2,1)S(1)}, bf16[1,256,128]{2,1,0:T(8,128)(2,1)S(1)}, u32[]{:S(2)}, u32[]{:S(2)}) collective-permute-start(bf16[1,256,128]{2,1,0:T(8,128)(2,1)S(1)} %get-tuple-element.45), channel_id=1, source_target_pairs={{0,8},{8,16},{16,24},{1,9},{9,17},{17,25},{2,10},{10,18},{18,26},{... | collective-permute-start | bytes 196616 | tf_op jit(solution)/shard_map/ppermute | solution.py:18
  194.6 5.5 %collective-permute-start.10 = (bf16[18,1,128]{2,1,0:T(2,128)(2,1)S(1)}, bf16[18,1,128]{2,1,0:T(2,128)(2,1)S(1)}, u32[]{:S(2)}, u32[]{:S(2)}) collective-permute-start(bf16[18,1,128]{2,1,0:T(2,128)(2,1)S(1)} %get-tuple-element.32), channel_id=1, source_target_pairs={{0,1},{1,2},{2,3},{3,4},{4,5},{5,6},{6,7},{8,9},{9,10},{10,11},{11... | collective-permute-start | bytes 13832 | tf_op jit(solution)/shard_map/ppermute | solution.py:18
  205.6 1.9 multiply_convert_fusion.4
  208.8 4.9 %collective-permute-start.12 = (bf16[1,256,128]{2,1,0:T(8,128)(2,1)S(1)}, bf16[1,256,128]{2,1,0:T(8,128)(2,1)S(1)}, u32[]{:S(2)}, u32[]{:S(2)}) collective-permute-start(bf16[1,256,128]{2,1,0:T(8,128)(2,1)S(1)} %get-tuple-element.43), channel_id=1, source_target_pairs={{0,8},{8,16},{16,24},{1,9},{9,17},{17,25},{2,10},{10,18},{18,26},{... | collective-permute-start | bytes 196616 | tf_op jit(solution)/shard_map/ppermute | solution.py:18
  215.9 5.7 %collective-permute-start.14 = (bf16[18,1,128]{2,1,0:T(2,128)(2,1)S(1)}, bf16[18,1,128]{2,1,0:T(2,128)(2,1)S(1)}, u32[]{:S(2)}, u32[]{:S(2)}) collective-permute-start(bf16[18,1,128]{2,1,0:T(2,128)(2,1)S(1)} %get-tuple-element.28), channel_id=1, source_target_pairs={{0,1},{1,2},{2,3},{3,4},{4,5},{5,6},{6,7},{8,9},{9,10},{10,11},{11... | collective-permute-start | bytes 13832 | tf_op jit(solution)/shard_map/ppermute | solution.py:18
  230.5 5.3 %collective-permute-start.16 = (bf16[1,256,128]{2,1,0:T(8,128)(2,1)S(1)}, bf16[1,256,128]{2,1,0:T(8,128)(2,1)S(1)}, u32[]{:S(2)}, u32[]{:S(2)}) collective-permute-start(bf16[1,256,128]{2,1,0:T(8,128)(2,1)S(1)} %get-tuple-element.41), channel_id=1, source_target_pairs={{0,8},{8,16},{16,24},{1,9},{9,17},{17,25},{2,10},{10,18},{18,26},{... | collective-permute-start | bytes 196616 | tf_op jit(solution)/shard_map/ppermute | solution.py:18
  238.0 5.9 %collective-permute-start.18 = (bf16[18,1,128]{2,1,0:T(2,128)(2,1)S(1)}, bf16[18,1,128]{2,1,0:T(2,128)(2,1)S(1)}, u32[]{:S(2)}, u32[]{:S(2)}) collective-permute-start(bf16[18,1,128]{2,1,0:T(2,128)(2,1)S(1)} %get-tuple-element.24), channel_id=1, source_target_pairs={{0,1},{1,2},{2,3},{3,4},{4,5},{5,6},{6,7},{8,9},{9,10},{10,11},{11... | collective-permute-start | bytes 13832 | tf_op jit(solution)/shard_map/ppermute | solution.py:18
  249.3 2.4 convolution_convert_fusion
  251.7 18.8 %fusion.7 = bf16[128,64,128]{2,1,0:T(8,128)(2,1)} fusion(bf16[128,256,128]{2,0,1:T(8,128)(2,1)S(1)} %convolution_convert_fusion, s32[128,64]{1,0:T(8,128)S(1)} %get-tuple-element.52), kind=kOutput, calls=%fused_computation.29 | convolution fusion | flops 540016640 | bytes 10518528 | tf_op jit(solution)/shard_map/sed,sec->sdc/dot_general | solution.py:147
  270.5 14.6 %all-to-all-start.2 = ((bf16[128,64,128]{2,1,0:T(8,128)(2,1)}), bf16[128,64,128]{2,1,0:T(8,128)(2,1)}, u32[]{:S(2)}, u32[]{:S(2)}) async-start(bf16[128,64,128]{2,1,0:T(8,128)(2,1)} %fusion.7), calls=%async_computation.2 | async-start | bytes 4194304 | tf_op jit(solution)/shard_map/all_to_all | solution.py:150
  285.2 50.0 %all-to-all-done.2 = bf16[128,64,128]{2,1,0:T(8,128)(2,1)} async-done(((bf16[128,64,128]{2,1,0:T(8,128)(2,1)}), bf16[128,64,128]{2,1,0:T(8,128)(2,1)}, u32[]{:S(2)}, u32[]{:S(2)}) %all-to-all-start.2) | async-done | bytes 2097184 | tf_op jit(solution)/shard_map/all_to_all | solution.py:150
  335.3 2.3 gather_fusion
  337.6 2.5 convolution_convert_fusion.2
  340.1 2.1 convolution_convert_fusion.1
  342.3 3.9 %copy.39 = bf16[4,16,128,128]{3,2,1,0:T(8,128)(2,1)} copy(bf16[4,16,128,128]{2,3,1,0:T(8,128)(2,1)} %bitcast.290) | data formatting | bytes 4194304
  (168 shorter events, 77.9 us)
Async XLA Ops:
  0.6 13.6 %copy-start = (bf16[4,16,128,128]{3,2,1,0:T(8,128)(2,1)S(1)}, bf16[4,16,128,128]{3,2,1,0:T(8,128)(2,1)}, u32[]{:S(2)}) copy-start(bf16[4,16,128,128]{3,2,1,0:T(8,128)(2,1)} %param.8) | copy-start | bytes 6291460
  5.4 12.7 %copy-start.8 = (s32[64]{0:T(128)}, s32[64]{0:T(128)S(1)}, u32[]{:S(2)}) copy-start(s32[64]{0:T(128)S(1)} %fusion.222) | copy-start | bytes 772
  6.9 19.2 %all-to-all-start = ((s32[32,1,256]{2,1,0:T(1,128)}), s32[32,1,256]{2,1,0:T(1,128)S(1)}, u32[]{:S(2)}, u32[]{:S(2)}) async-start(s32[32,1,256]{2,1,0:T(1,128)} %reshape.505), calls=%async_computation | async-start | bytes 65536 | tf_op jit(solution)/shard_map/all_to_all | solution.py:96
  26.2 56.0 %all-to-all-start.1 = ((bf16[128,64,128]{2,1,0:T(8,128)(2,1)}), bf16[128,64,128]{2,1,0:T(8,128)(2,1)}, u32[]{:S(2)}, u32[]{:S(2)}) async-start(bf16[128,64,128]{2,1,0:T(8,128)(2,1)} %scatter_fusion), calls=%async_computation.1 | async-start | bytes 4194304 | tf_op jit(solution)/shard_map/all_to_all | solution.py:95
  106.0 4.7 %copy-start.6 = (bf16[4,3,3,128,128]{4,3,2,1,0:T(8,128)(2,1)S(1)}, bf16[4,3,3,128,128]{4,3,2,1,0:T(8,128)(2,1)}, u32[]{:S(2)}) copy-start(bf16[4,3,3,128,128]{4,3,2,1,0:T(8,128)(2,1)} %param.12) | copy-start | bytes 3538948
  106.1 5.0 %collective-permute-start.1 = (bf16[4,256,128]{2,1,0:T(8,128)(2,1)S(1)}, bf16[4,256,128]{2,1,0:T(8,128)(2,1)S(1)}, u32[]{:S(2)}, u32[]{:S(2)}) collective-permute-start(bf16[4,256,128]{2,1,0:T(8,128)(2,1)S(1)} %bitcast.298), channel_id=1, source_target_pairs={{8,0},{16,8},{24,16},{9,1},{17,9},{25,17},{10,2},{18,10},{26,18},{... | collective-permute-start | bytes 786440 | tf_op jit(solution)/shard_map/ppermute | solution.py:20
  107.6 4.2 %collective-permute-start = (bf16[4,256,128]{2,1,0:T(8,128)(2,1)S(1)}, bf16[4,256,128]{2,1,0:T(8,128)(2,1)S(1)}, u32[]{:S(2)}, u32[]{:S(2)}) collective-permute-start(bf16[4,256,128]{2,1,0:T(8,128)(2,1)S(1)} %bitcast.299), channel_id=1, source_target_pairs={{0,8},{8,16},{16,24},{1,9},{9,17},{17,25},{2,10},{10,18},{18,26},{... | collective-permute-start | bytes 786440 | tf_op jit(solution)/shard_map/ppermute | solution.py:18
  110.8 17.2 %copy-start.4 = (bf16[3,3,128,128]{3,2,1,0:T(8,128)(2,1)}, bf16[3,3,128,128]{3,2,1,0:T(8,128)(2,1)S(1)}, u32[]{:S(2)}) copy-start(bf16[3,3,128,128]{3,2,1,0:T(8,128)(2,1)S(1)} %get-tuple-element.39) | copy-start | bytes 884740
  111.8 5.9 %collective-permute-start.3 = (bf16[24,4,128]{2,1,0:T(4,128)(2,1)S(1)}, bf16[24,4,128]{2,1,0:T(4,128)(2,1)S(1)}, u32[]{:S(2)}, u32[]{:S(2)}) collective-permute-start(bf16[24,4,128]{2,1,0:T(4,128)(2,1)S(1)} %get-tuple-element.20), channel_id=1, source_target_pairs={{1,0},{2,1},{3,2},{4,3},{5,4},{6,5},{7,6},{9,8},{10,9},{11,10},{12... | collective-permute-start | bytes 73736 | tf_op jit(solution)/shard_map/ppermute | solution.py:20
  113.1 6.1 %collective-permute-start.2 = (bf16[24,4,128]{2,1,0:T(4,128)(2,1)S(1)}, bf16[24,4,128]{2,1,0:T(4,128)(2,1)S(1)}, u32[]{:S(2)}, u32[]{:S(2)}) collective-permute-start(bf16[24,4,128]{2,1,0:T(4,128)(2,1)S(1)} %get-tuple-element.19), channel_id=1, source_target_pairs={{0,1},{1,2},{2,3},{3,4},{4,5},{5,6},{6,7},{8,9},{9,10},{10,11},{11... | collective-permute-start | bytes 73736 | tf_op jit(solution)/shard_map/ppermute | solution.py:18
  165.8 6.2 %collective-permute-start.5 = (bf16[1,256,128]{2,1,0:T(8,128)(2,1)S(1)}, bf16[1,256,128]{2,1,0:T(8,128)(2,1)S(1)}, u32[]{:S(2)}, u32[]{:S(2)}) collective-permute-start(bf16[1,256,128]{2,1,0:T(8,128)(2,1)S(1)} %get-tuple-element.48), channel_id=1, source_target_pairs={{8,0},{16,8},{24,16},{9,1},{17,9},{25,17},{10,2},{18,10},{26,18},{... | collective-permute-start | bytes 196616 | tf_op jit(solution)/shard_map/ppermute | solution.py:20
  167.1 5.3 %collective-permute-start.4 = (bf16[1,256,128]{2,1,0:T(8,128)(2,1)S(1)}, bf16[1,256,128]{2,1,0:T(8,128)(2,1)S(1)}, u32[]{:S(2)}, u32[]{:S(2)}) collective-permute-start(bf16[1,256,128]{2,1,0:T(8,128)(2,1)S(1)} %get-tuple-element.47), channel_id=1, source_target_pairs={{0,8},{8,16},{16,24},{1,9},{9,17},{17,25},{2,10},{10,18},{18,26},{... | collective-permute-start | bytes 196616 | tf_op jit(solution)/shard_map/ppermute | solution.py:18
  172.5 7.2 %collective-permute-start.7 = (bf16[18,1,128]{2,1,0:T(2,128)(2,1)S(1)}, bf16[18,1,128]{2,1,0:T(2,128)(2,1)S(1)}, u32[]{:S(2)}, u32[]{:S(2)}) collective-permute-start(bf16[18,1,128]{2,1,0:T(2,128)(2,1)S(1)} %get-tuple-element.35), channel_id=1, source_target_pairs={{1,0},{2,1},{3,2},{4,3},{5,4},{6,5},{7,6},{9,8},{10,9},{11,10},{12... | collective-permute-start | bytes 13832 | tf_op jit(solution)/shard_map/ppermute | solution.py:20
  173.8 5.9 %collective-permute-start.6 = (bf16[18,1,128]{2,1,0:T(2,128)(2,1)S(1)}, bf16[18,1,128]{2,1,0:T(2,128)(2,1)S(1)}, u32[]{:S(2)}, u32[]{:S(2)}) collective-permute-start(bf16[18,1,128]{2,1,0:T(2,128)(2,1)S(1)} %get-tuple-element.36), channel_id=1, source_target_pairs={{0,1},{1,2},{2,3},{3,4},{4,5},{5,6},{6,7},{8,9},{9,10},{10,11},{11... | collective-permute-start | bytes 13832 | tf_op jit(solution)/shard_map/ppermute | solution.py:18
  184.5 8.2 %collective-permute-start.9 = (bf16[1,256,128]{2,1,0:T(8,128)(2,1)S(1)}, bf16[1,256,128]{2,1,0:T(8,128)(2,1)S(1)}, u32[]{:S(2)}, u32[]{:S(2)}) collective-permute-start(bf16[1,256,128]{2,1,0:T(8,128)(2,1)S(1)} %get-tuple-element.46), channel_id=1, source_target_pairs={{8,0},{16,8},{24,16},{9,1},{17,9},{25,17},{10,2},{18,10},{26,18},{... | collective-permute-start | bytes 196616 | tf_op jit(solution)/shard_map/ppermute | solution.py:20
  185.8 7.4 %collective-permute-start.8 = (bf16[1,256,128]{2,1,0:T(8,128)(2,1)S(1)}, bf16[1,256,128]{2,1,0:T(8,128)(2,1)S(1)}, u32[]{:S(2)}, u32[]{:S(2)}) collective-permute-start(bf16[1,256,128]{2,1,0:T(8,128)(2,1)S(1)} %get-tuple-element.45), channel_id=1, source_target_pairs={{0,8},{8,16},{16,24},{1,9},{9,17},{17,25},{2,10},{10,18},{18,26},{... | collective-permute-start | bytes 196616 | tf_op jit(solution)/shard_map/ppermute | solution.py:18
  193.3 7.7 %collective-permute-start.11 = (bf16[18,1,128]{2,1,0:T(2,128)(2,1)S(1)}, bf16[18,1,128]{2,1,0:T(2,128)(2,1)S(1)}, u32[]{:S(2)}, u32[]{:S(2)}) collective-permute-start(bf16[18,1,128]{2,1,0:T(2,128)(2,1)S(1)} %get-tuple-element.31), channel_id=1, source_target_pairs={{1,0},{2,1},{3,2},{4,3},{5,4},{6,5},{7,6},{9,8},{10,9},{11,10},{12... | collective-permute-start | bytes 13832 | tf_op jit(solution)/shard_map/ppermute | solution.py:20
  194.6 6.8 %collective-permute-start.10 = (bf16[18,1,128]{2,1,0:T(2,128)(2,1)S(1)}, bf16[18,1,128]{2,1,0:T(2,128)(2,1)S(1)}, u32[]{:S(2)}, u32[]{:S(2)}) collective-permute-start(bf16[18,1,128]{2,1,0:T(2,128)(2,1)S(1)} %get-tuple-element.32), channel_id=1, source_target_pairs={{0,1},{1,2},{2,3},{3,4},{4,5},{5,6},{6,7},{8,9},{9,10},{10,11},{11... | collective-permute-start | bytes 13832 | tf_op jit(solution)/shard_map/ppermute | solution.py:18
  203.8 1.8 copy-start.2
  207.5 6.6 %collective-permute-start.13 = (bf16[1,256,128]{2,1,0:T(8,128)(2,1)S(1)}, bf16[1,256,128]{2,1,0:T(8,128)(2,1)S(1)}, u32[]{:S(2)}, u32[]{:S(2)}) collective-permute-start(bf16[1,256,128]{2,1,0:T(8,128)(2,1)S(1)} %get-tuple-element.44), channel_id=1, source_target_pairs={{8,0},{16,8},{24,16},{9,1},{17,9},{25,17},{10,2},{18,10},{26,18},{... | collective-permute-start | bytes 196616 | tf_op jit(solution)/shard_map/ppermute | solution.py:20
  208.8 5.8 %collective-permute-start.12 = (bf16[1,256,128]{2,1,0:T(8,128)(2,1)S(1)}, bf16[1,256,128]{2,1,0:T(8,128)(2,1)S(1)}, u32[]{:S(2)}, u32[]{:S(2)}) collective-permute-start(bf16[1,256,128]{2,1,0:T(8,128)(2,1)S(1)} %get-tuple-element.43), channel_id=1, source_target_pairs={{0,8},{8,16},{16,24},{1,9},{9,17},{17,25},{2,10},{10,18},{18,26},{... | collective-permute-start | bytes 196616 | tf_op jit(solution)/shard_map/ppermute | solution.py:18
  214.6 7.9 %collective-permute-start.15 = (bf16[18,1,128]{2,1,0:T(2,128)(2,1)S(1)}, bf16[18,1,128]{2,1,0:T(2,128)(2,1)S(1)}, u32[]{:S(2)}, u32[]{:S(2)}) collective-permute-start(bf16[18,1,128]{2,1,0:T(2,128)(2,1)S(1)} %get-tuple-element.27), channel_id=1, source_target_pairs={{1,0},{2,1},{3,2},{4,3},{5,4},{6,5},{7,6},{9,8},{10,9},{11,10},{12... | collective-permute-start | bytes 13832 | tf_op jit(solution)/shard_map/ppermute | solution.py:20
  215.9 7.1 %collective-permute-start.14 = (bf16[18,1,128]{2,1,0:T(2,128)(2,1)S(1)}, bf16[18,1,128]{2,1,0:T(2,128)(2,1)S(1)}, u32[]{:S(2)}, u32[]{:S(2)}) collective-permute-start(bf16[18,1,128]{2,1,0:T(2,128)(2,1)S(1)} %get-tuple-element.28), channel_id=1, source_target_pairs={{0,1},{1,2},{2,3},{3,4},{4,5},{5,6},{6,7},{8,9},{9,10},{10,11},{11... | collective-permute-start | bytes 13832 | tf_op jit(solution)/shard_map/ppermute | solution.py:18
  225.5 1.8 copy-start.1
  227.3 8.5 %copy-start.5 = (bf16[3,3,128,128]{3,2,1,0:T(8,128)(2,1)S(1)}, bf16[3,3,128,128]{3,2,1,0:T(8,128)(2,1)}, u32[]{:S(2)}) copy-start(bf16[3,3,128,128]{3,2,1,0:T(8,128)(2,1)} %copy-done.4) | copy-start | bytes 884740
  229.2 7.1 %collective-permute-start.17 = (bf16[1,256,128]{2,1,0:T(8,128)(2,1)S(1)}, bf16[1,256,128]{2,1,0:T(8,128)(2,1)S(1)}, u32[]{:S(2)}, u32[]{:S(2)}) collective-permute-start(bf16[1,256,128]{2,1,0:T(8,128)(2,1)S(1)} %get-tuple-element.42), channel_id=1, source_target_pairs={{8,0},{16,8},{24,16},{9,1},{17,9},{25,17},{10,2},{18,10},{26,18},{... | collective-permute-start | bytes 196616 | tf_op jit(solution)/shard_map/ppermute | solution.py:20
  230.5 6.2 %collective-permute-start.16 = (bf16[1,256,128]{2,1,0:T(8,128)(2,1)S(1)}, bf16[1,256,128]{2,1,0:T(8,128)(2,1)S(1)}, u32[]{:S(2)}, u32[]{:S(2)}) collective-permute-start(bf16[1,256,128]{2,1,0:T(8,128)(2,1)S(1)} %get-tuple-element.41), channel_id=1, source_target_pairs={{0,8},{8,16},{16,24},{1,9},{9,17},{17,25},{2,10},{10,18},{18,26},{... | collective-permute-start | bytes 196616 | tf_op jit(solution)/shard_map/ppermute | solution.py:18
  236.7 8.1 %collective-permute-start.19 = (bf16[18,1,128]{2,1,0:T(2,128)(2,1)S(1)}, bf16[18,1,128]{2,1,0:T(2,128)(2,1)S(1)}, u32[]{:S(2)}, u32[]{:S(2)}) collective-permute-start(bf16[18,1,128]{2,1,0:T(2,128)(2,1)S(1)} %get-tuple-element.23), channel_id=1, source_target_pairs={{1,0},{2,1},{3,2},{4,3},{5,4},{6,5},{7,6},{9,8},{10,9},{11,10},{12... | collective-permute-start | bytes 13832 | tf_op jit(solution)/shard_map/ppermute | solution.py:20
  238.0 7.1 %collective-permute-start.18 = (bf16[18,1,128]{2,1,0:T(2,128)(2,1)S(1)}, bf16[18,1,128]{2,1,0:T(2,128)(2,1)S(1)}, u32[]{:S(2)}, u32[]{:S(2)}) collective-permute-start(bf16[18,1,128]{2,1,0:T(2,128)(2,1)S(1)} %get-tuple-element.24), channel_id=1, source_target_pairs={{0,1},{1,2},{2,3},{3,4},{4,5},{5,6},{6,7},{8,9},{9,10},{10,11},{11... | collective-permute-start | bytes 13832 | tf_op jit(solution)/shard_map/ppermute | solution.py:18
  270.5 14.7 %copy-start.9 = (s32[64]{0:T(128)S(1)}, s32[64]{0:T(128)}, u32[]{:S(2)}) copy-start(s32[64]{0:T(128)} %copy-done.8) | copy-start | bytes 772
  270.5 64.7 %all-to-all-start.2 = ((bf16[128,64,128]{2,1,0:T(8,128)(2,1)}), bf16[128,64,128]{2,1,0:T(8,128)(2,1)}, u32[]{:S(2)}, u32[]{:S(2)}) async-start(bf16[128,64,128]{2,1,0:T(8,128)(2,1)} %fusion.7), calls=%async_computation.2 | async-start | bytes 4194304 | tf_op jit(solution)/shard_map/all_to_all | solution.py:150
  337.6 2.5 copy-start.3
  (1 other events, 1.2 us)
where the time goes:
time: 351 us; the launch traced here: 346 us
  matrix products  117 us (33%)
  waiting for transfers between devices  103 us (29%)
  starting transfers between devices  91.8 us (26%)
  local copies, waits for them, and re-layouts  23.5 us (7%)
  other arithmetic  8.67 us (2%)
    ppermute x10, starting transfers between devices, extended(): lax.ppermute(tail, axis, [(i, (i + 1) % count) for i in range(ends)])  50.8 us
    all_to_all x1, waiting for transfers between devices, per_device(): lax.all_to_all(grad_rows, ('cam', 'tile'), split_axis=0, concat_axis=0, t...  50 us
    all_to_all x1, waiting for transfers between devices, per_device(): lax.all_to_all(send_rows, ('cam', 'tile'), split_axis=0, concat_axis=0, t...  48.1 us
    dot_general x36, matrix products, conv_taps(): jnp.einsum('xyi,io->xyo', window, kernel[row_tap, col_tap], preferred_ele...  45 us
    dot_general x36, matrix products, conv_taps(): jnp.einsum('xyo,io->xyi', window, kernel[2 - row_tap, 2 - col_tap], prefe...  20.8 us
    dot_general x1, matrix products, per_device(): jnp.einsum('sed,sec->sdc', cell_onehot, slot_grad, preferred_element_type...  18.8 us
    dot_general x1, matrix products, per_device(): jnp.einsum('ts,sec->tec', tile_onehot.astype(jnp.float32), slot_sums, pre...  15.1 us
    all_to_all x1, starting transfers between devices, per_device(): lax.all_to_all(grad_rows, ('cam', 'tile'), split_axis=0, concat_axis=0, t...  14.6 us
  transfers between devices with their start and end apart: 23, of which 12 were waited for; matrix products, arithmetic and copies ran while one was open for 6% of the time, Pallas kernels for 0%

commit v1 on v0

v1 whole, which is shorter than its diff:
```python
import functools

import jax
import jax.numpy as jnp
from jax import lax
from jax.experimental import pallas as pl
from jax.experimental.pallas import tpu as pltpu
from jax.sharding import PartitionSpec as P

TS = 16
LAYERS = 4
ROW_HALO = 2 * LAYERS
COL_HALO = 16
META_ROWS = 16
MESH = pl.DeviceIdType.MESH
BF = jnp.bfloat16
F32 = jnp.float32
DIRECTIONS = [(dx, dy) for dx in (-1, 0, 1) for dy in (-1, 0, 1) if (dx, dy) != (0, 0)]


def lift_kernel(cap, bins, owner_ref, meta_ref, depth_ref, context_ref, send_ref, count, meta_rows):
    step = pl.program_id(0)
    owners = send_ref.shape[0]
    blocks = depth_ref.shape[0]

    @pl.when(step == 0)
    def _():
        meta_rows[...] = jnp.zeros_like(meta_rows)

        def clear(o, carry):
            count[o] = 0
            return carry

        lax.fori_loop(0, owners, clear, 0)

    for b in range(blocks):
        owner = owner_ref[step * blocks + b]
        rank = count[owner]
        count[owner] = rank + 1
        lifted = jnp.dot(depth_ref[b], context_ref[b], preferred_element_type=F32).astype(BF)
        send_ref[owner, pl.ds(pl.multiple_of(rank * bins, bins), bins), :] = lifted
        meta_rows[owner, pl.ds(rank, 1), :] = meta_ref[pl.ds(b, 1), :]

    @pl.when(step == pl.num_programs(0) - 1)
    def _():
        def put(o, carry):
            rows = meta_rows[o]
            send_ref[o, cap * bins : cap * bins + META_ROWS, :] = jnp.concatenate(
                [rows, jnp.zeros_like(rows)], axis=0
            ).astype(BF)
            return carry

        lax.fori_loop(0, owners, put, 0)


def lift(depth, context, owner, meta, owners, cap):
    blocks, bins, pixels = depth.shape
    channels = context.shape[2]
    chunk = 16
    rows = cap * bins + META_ROWS
    return pl.pallas_call(
        functools.partial(lift_kernel, cap, bins),
        grid=(blocks // chunk,),
        out_shape=jax.ShapeDtypeStruct((owners, rows, channels), BF),
        in_specs=[
            pl.BlockSpec(memory_space=pltpu.SMEM),
            pl.BlockSpec((chunk, 128), lambda i: (i, 0)),
            pl.BlockSpec((chunk, bins, pixels), lambda i: (i, 0, 0)),
            pl.BlockSpec((chunk, pixels, channels), lambda i: (i, 0, 0)),
        ],
        out_specs=pl.BlockSpec((owners, rows, channels), lambda i: (0, 0, 0)),
        scratch_shapes=[pltpu.SMEM((owners,), jnp.int32), pltpu.VMEM((owners, 8, 128), F32)],
        compiler_params=pltpu.CompilerParams(vmem_limit_bytes=40 << 20),
        name="lift",
    )(owner, meta, depth, context)


def splat_kernel(cap, bins, tile_ref, valid_ref, recv_ref, out_ref, sums):
    owners = recv_ref.shape[0]
    tiles = sums.shape[0]
    cells = TS * TS
    sums[...] = jnp.zeros_like(sums)

    def source(o, carry):
        def pair(first):
            meta = recv_ref[o, cap * bins : cap * bins + META_ROWS, :].astype(F32)
            parts = []
            for k in (first, first + 1):
                row = meta[k : k + 1, 0:bins]
                live = meta[k : k + 1, bins + 1 : bins + 2] > 0.5
                place = jnp.where(live, row, -1.0)
                wide = jnp.broadcast_to(place, (cells, bins))
                index = lax.broadcasted_iota(jnp.int32, (cells, bins), 0).astype(F32)
                hot = jnp.where(wide == index, 1.0, 0.0).astype(BF)
                rows = recv_ref[o, k * bins : (k + 1) * bins, :]
                rows = jnp.where(jnp.broadcast_to(live, rows.shape), rows.astype(F32), 0.0).astype(BF)
                parts.append(jnp.dot(hot, rows, preferred_element_type=F32))
            for k, part in zip((first, first + 1), parts):
                tile = tile_ref[o * cap + k]
                sums[tile] = sums[tile] + part

        for first in range(0, cap, 2):
            @pl.when(valid_ref[o * cap + first] > 0)
            def _():
                pair(first)

        return carry

    lax.fori_loop(0, owners, source, 0)
    for tile in range(tiles):
        for row in range(TS):
            out_ref[row, tile * TS : (tile + 1) * TS, :] = sums[
                tile, row * TS : (row + 1) * TS, :
            ].astype(BF)


def splat(received, slot_tile, slot_valid, cap, bins, rows, cols):
    channels = received.shape[2]
    tiles = (rows // TS) * (cols // TS)
    return pl.pallas_call(
        functools.partial(splat_kernel, cap, bins),
        out_shape=jax.ShapeDtypeStruct((rows, cols, channels), BF),
        in_specs=[
            pl.BlockSpec(memory_space=pltpu.SMEM),
            pl.BlockSpec(memory_space=pltpu.SMEM),
            pl.BlockSpec(memory_space=pltpu.VMEM),
        ],
        out_specs=pl.BlockSpec(memory_space=pltpu.VMEM),
        scratch_shapes=[pltpu.VMEM((tiles, TS * TS, channels), F32)],
        compiler_params=pltpu.CompilerParams(vmem_limit_bytes=40 << 20),
        name="splat",
    )(slot_tile, slot_valid, received)


def halo_kernel(cams, tiles, h_ref, g_ref, hp_ref, gp_ref, send_sem, recv_sem, local_sem):
    cam = lax.axis_index("cam")
    tile = lax.axis_index("tile")
    rows, cols = h_ref.shape[0], h_ref.shape[1]

    def there(dx, dy):
        ok = None
        for at, step, count in ((cam, dx, cams), (tile, dy, tiles)):
            if step:
                here = (at + step >= 0) & (at + step < count)
                ok = here if ok is None else ok & here
        return ok

    barrier = pltpu.get_barrier_semaphore()
    arrivals = 0
    for dx, dy in DIRECTIONS:
        near = there(dx, dy)
        arrivals = arrivals + near.astype(jnp.int32)

        @pl.when(near)
        def _():
            pl.semaphore_signal(
                barrier, inc=1, device_id=(cam + dx, tile + dy), device_id_type=MESH
            )

    pl.semaphore_wait(barrier, arrivals)

    def copies(index):
        dx, dy = DIRECTIONS[index]
        made = []
        for which, (source, target, halo) in enumerate(
            ((h_ref, hp_ref, ROW_HALO), (g_ref, gp_ref, LAYERS))
        ):
            row_src, row_dst, row_len = {
                -1: (0, halo + rows, halo),
                0: (0, halo, rows),
                1: (rows - halo, 0, halo),
            }[dx]
            col_src, col_dst, col_len = {
                -1: (0, COL_HALO + cols, COL_HALO),
                0: (0, COL_HALO, cols),
                1: (cols - COL_HALO, 0, COL_HALO),
            }[dy]
            made.append(
                pltpu.make_async_remote_copy(
                    src_ref=source.at[pl.ds(row_src, row_len), pl.ds(col_src, col_len)],
                    dst_ref=target.at[pl.ds(row_dst, row_len), pl.ds(col_dst, col_len)],
                    send_sem=send_sem.at[2 * index + which],
                    recv_sem=recv_sem.at[2 * index + which],
                    device_id=(cam + dx, tile + dy),
                    device_id_type=MESH,
                )
            )
        return made

    for index in range(len(DIRECTIONS)):
        @pl.when(there(*DIRECTIONS[index]))
        def _():
            for copy in copies(index):
                copy.start()

    own = [
        pltpu.make_async_copy(
            source, target.at[pl.ds(halo, rows), pl.ds(COL_HALO, cols)], local_sem.at[which]
        )
        for which, (source, target, halo) in enumerate(
            ((h_ref, hp_ref, ROW_HALO), (g_ref, gp_ref, LAYERS))
        )
    ]
    for copy in own:
        copy.start()
    for index, (dx, dy) in enumerate(DIRECTIONS):
        @pl.when(there(dx, dy))
        def _():
            for copy in copies(index):
                copy.wait_send()

        @pl.when(there(-dx, -dy))
        def _():
            for copy in copies(index):
                copy.wait_recv()
    for copy in own:
        copy.wait()


def halo_exchange(cells, cotangent, cams, tiles):
    rows, cols, channels = cells.shape
    wide = cols + 2 * COL_HALO
    anywhere = pl.BlockSpec(memory_space=pl.ANY)
    return pl.pallas_call(
        functools.partial(halo_kernel, cams, tiles),
        out_shape=[
            jax.ShapeDtypeStruct((rows + 2 * ROW_HALO, wide, channels), BF),
            jax.ShapeDtypeStruct((rows + 2 * LAYERS, wide, channels), BF),
        ],
        in_specs=[anywhere] * 2,
        out_specs=[anywhere] * 2,
        scratch_shapes=[
            pltpu.SemaphoreType.DMA((2 * len(DIRECTIONS),)),
            pltpu.SemaphoreType.DMA((2 * len(DIRECTIONS),)),
            pltpu.SemaphoreType.DMA((2,)),
        ],
        compiler_params=pltpu.CompilerParams(collective_id=0, has_side_effects=True),
        name="halo",
    )(cells, cotangent)


def conv_kernel(
    cap, bins, grid_rows, grid_cols,
    tile_ref, valid_ref, hp_ref, gp_ref, weight_ref, cells_ref,
    out_ref, back_ref,
    fields, slopes, masks, wide_weight, grads,
):
    rows, cols = out_ref.shape[0], out_ref.shape[1]
    channels = out_ref.shape[2]
    width = hp_ref.shape[1]
    tall = hp_ref.shape[0]
    row_first = lax.axis_index("cam") * rows - ROW_HALO
    col_first = lax.axis_index("tile") * cols - COL_HALO
    column = lax.broadcasted_iota(jnp.int32, (width, channels), 0) + col_first
    masks[0] = jnp.zeros((width, channels), F32)
    masks[1] = jnp.where((column >= 0) & (column < grid_cols), 1.0, 0.0)
    wide_weight[...] = jnp.zeros_like(wide_weight)

    def mask_of(row):
        at = row + row_first
        return masks[((at >= 0) & (at < grid_rows)).astype(jnp.int32)]

    def clean(row, carry):
        fields[0, row] = jnp.where(mask_of(row) > 0.5, hp_ref[row].astype(F32), 0.0).astype(BF)
        return carry

    lax.fori_loop(0, tall, clean, 0)

    def spread(index):
        slot = index % 2
        for j in range(2):
            for s in range(3):
                for r in range(3):
                    k = r + j
                    wide_weight[
                        slot,
                        k * channels : (k + 1) * channels,
                        (j * 3 + s) * channels : (j * 3 + s + 1) * channels,
                    ] = weight_ref[index, r, s]

    def sweep(index, source, first, last, finish):
        spread(index)

        def one(row):
            window = jnp.concatenate([fields[source, row - 1 + k] for k in range(4)], axis=1)
            taps = jnp.dot(window, wide_weight[index % 2], preferred_element_type=F32)
            for j in range(2):
                base = j * 3 * channels
                left = taps[:, base : base + channels]
                middle = taps[:, base + channels : base + 2 * channels]
                right = taps[:, base + 2 * channels : base + 3 * channels]
                finish(
                    row + j,
                    pltpu.roll(left, 1, 0) + middle + pltpu.roll(right, width - 1, 0),
                )

        pairs = (last - first) // 2

        def two(step, carry):
            one(first + 4 * step)
            one(first + 4 * step + 2)
            return carry

        lax.fori_loop(0, pairs // 2, two, 0)
        if pairs % 2:
            one(last - 2)

    for layer in range(1, LAYERS + 1):
        def finish_forward(row, pre, layer=layer):
            sigma = 0.5 * jnp.tanh(0.5 * pre) + 0.5
            value = pre * sigma
            slope = sigma * (1.0 + pre * (1.0 - sigma))
            if layer < LAYERS:
                slopes[layer - 1, row] = slope
                fields[layer % 2, row] = (value * mask_of(row)).astype(BF)
            else:
                grad = gp_ref[row - LAYERS].astype(F32)
                grad = jnp.where(mask_of(row) > 0.5, grad, 0.0)
                fields[layer % 2, row] = (grad * slope).astype(BF)
                inner = jnp.clip(row - ROW_HALO, 0, rows - 1)

                @pl.when(inner == row - ROW_HALO)
                def _():
                    out_ref[inner] = value[COL_HALO : COL_HALO + cols].astype(BF)

        sweep(layer - 1, (layer - 1) % 2, layer, tall - layer, finish_forward)

    for layer in range(LAYERS, 0, -1):
        done = LAYERS - layer

        def finish_backward(row, grad, layer=layer, done=done):
            grad = grad.astype(BF)
            if layer > 1:
                fields[(done + 1) % 2, row] = (
                    grad.astype(F32) * slopes[layer - 2, row] * mask_of(row)
                ).astype(BF)
            else:
                inner = row - ROW_HALO
                for t in range(cols // TS):
                    grads[t, pl.ds(pl.multiple_of(inner * TS, TS), TS), :] = grad[
                        COL_HALO + t * TS : COL_HALO + (t + 1) * TS
                    ]

        sweep(
            LAYERS + layer - 1, done % 2,
            ROW_HALO + 1 - layer, ROW_HALO + rows - 1 + layer, finish_backward,
        )

    slots = cells_ref.shape[1]
    owners = slots // cap
    lane = lax.broadcasted_iota(jnp.int32, (bins, slots), 1)
    cell = lax.broadcasted_iota(jnp.int32, (bins, TS * TS), 1).astype(F32)

    def send_back(o, carry):
        def pair(first):
            for k in (first, first + 1):
                slot = o * cap + k
                place = jnp.sum(jnp.where(lane == slot, cells_ref[...], 0.0), axis=1, keepdims=True)
                hot = jnp.where(place == cell, 1.0, 0.0).astype(BF)
                back_ref[pl.ds(pl.multiple_of(slot * bins, bins), bins), :] = jnp.dot(
                    hot, grads[tile_ref[slot]], preferred_element_type=F32
                ).astype(BF)

        for first in range(0, cap, 2):
            @pl.when(valid_ref[o * cap + first] > 0)
            def _():
                pair(first)

        return carry

    lax.fori_loop(0, owners, send_back, 0)


def convolve(hp, gp, weights, slot_tile, slot_valid, cells, cap, bins, rows, cols, grid_shape):
    tall, wide, channels = hp.shape
    assert rows == TS
    vmem = pl.BlockSpec(memory_space=pltpu.VMEM)
    smem = pl.BlockSpec(memory_space=pltpu.SMEM)
    return pl.pallas_call(
        functools.partial(conv_kernel, cap, bins, *grid_shape),
        out_shape=[
            jax.ShapeDtypeStruct((rows, cols, channels), BF),
            jax.ShapeDtypeStruct((cells.shape[1] * bins, channels), BF),
        ],
        in_specs=[smem, smem, vmem, vmem, vmem, vmem],
        out_specs=[vmem, vmem],
        scratch_shapes=[
            pltpu.VMEM((2, tall, wide, channels), BF),
            pltpu.VMEM((LAYERS - 1, tall, wide, channels), F32),
            pltpu.VMEM((2, wide, channels), F32),
            pltpu.VMEM((2, 4 * channels, 6 * channels), BF),
            pltpu.VMEM((cols // TS, TS * TS, channels), BF),
        ],
        compiler_params=pltpu.CompilerParams(vmem_limit_bytes=56 << 20),
        name="convolutions",
    )(slot_tile, slot_valid, hp, gp, weights, cells)


def per_device(
    depth_weights, context, block_owner, block_local, block_cell, conv_weight, cotangent
):
    cams_here, blocks_cam, bins, pixels = depth_weights.shape
    channels = context.shape[3]
    rows, cols = cotangent.shape[0], cotangent.shape[1]
    cams = lax.axis_size("cam")
    tiles = lax.axis_size("tile")
    owners = cams * tiles
    blocks = cams_here * blocks_cam
    cap = max(2, 2 * blocks // owners)
    depth = depth_weights.reshape(blocks, bins, pixels)
    flat_context = context.reshape(blocks, pixels, channels)
    owner = block_owner.reshape(blocks)
    meta = jnp.concatenate(
        [
            block_cell.reshape(blocks, bins),
            block_local.reshape(blocks, 1),
            jnp.ones((blocks, 1), jnp.int32),
            jnp.zeros((blocks, 128 - bins - 2), jnp.int32),
        ],
        axis=1,
    ).astype(F32)
    sent = lift(depth, flat_context, owner, meta, owners, cap)
    received = lax.all_to_all(sent, ("cam", "tile"), split_axis=0, concat_axis=0, tiled=True)
    slot_meta = received[:, cap * bins : cap * bins + cap, :].reshape(owners * cap, 128)
    slot_tile = slot_meta[:, bins].astype(jnp.int32)
    slot_valid = slot_meta[:, bins + 1].astype(jnp.int32)
    slot_cells = slot_meta[:, :bins].astype(F32).T
    backward = jnp.swapaxes(conv_weight[:, ::-1, ::-1], 3, 4)
    weights = jnp.concatenate([conv_weight, backward], axis=0)
    cells = splat(received, slot_tile, slot_valid, cap, bins, rows, cols)
    hp, gp = halo_exchange(cells, cotangent, cams, tiles)
    bev_out, back = convolve(
        hp, gp, weights, slot_tile, slot_valid, slot_cells, cap, bins, rows, cols,
        (rows * cams, cols * tiles),
    )
    returned = lax.all_to_all(
        back.reshape(owners, cap * bins, channels),
        ("cam", "tile"), split_axis=0, concat_axis=0, tiled=True,
    ).reshape(owners * cap, bins, channels)
    positions = jnp.arange(blocks, dtype=jnp.int32)
    earlier = (owner[:, None] == owner[None, :]) & (positions[None, :] < positions[:, None])
    slot_index = owner * cap + jnp.sum(earlier.astype(jnp.int32), axis=1)
    block_grad = returned[slot_index]
    grad_context = jnp.einsum(
        "bdp,bdc->bpc", depth, block_grad, preferred_element_type=F32
    ).astype(BF)
    grad_depth = jnp.einsum(
        "bdc,bpc->bdp", block_grad, flat_context, preferred_element_type=F32
    ).astype(BF)
    return (
        bev_out,
        grad_depth.reshape(depth_weights.shape),
        grad_context.reshape(context.shape),
    )


def solution(mesh):
    placed = (
        P(("cam", "tile"), None, None, None),
        P(("cam", "tile"), None, None, None),
        P(("cam", "tile"), None, None),
        P(("cam", "tile"), None),
        P(("cam", "tile"), None, None),
        P(),
        P("cam", "tile", None),
    )
    return jax.shard_map(
        per_device,
        mesh=mesh,
        in_specs=placed,
        out_specs=(
            P("cam", "tile", None),
            P(("cam", "tile"), None, None, None),
            P(("cam", "tile"), None, None, None),
        ),
        check_vma=False,
    )
```

time: 351 us -> 276 us (0.79); the launches traced: 346 us -> 276 us
  Pallas kernels: 0 us -> 126 us
  matrix products: 117 us -> 4.64 us
  starting transfers between devices: 91.8 us -> 24.7 us
  local copies, waits for them, and re-layouts: 23.5 us -> 17.4 us
  waiting for transfers between devices: 103 us -> 98.1 us
  other arithmetic: 8.67 us -> 4.79 us
    pallas_call x0 -> x4, Pallas kernels: none -> 126 us  [the longest x1 65.6 us: halo_exchange(): pl.pallas_call(functools.partial(halo_kernel, cams, tiles), out_shape=[ja...]
    dot_general x78 -> x1, matrix products: 115 us -> 2.11 us  [per_device(): jnp.einsum('bdp,bdc->bpc', depth, block_grad, preferred_element_type=F32)]
    ppermute x20 -> x0, starting transfers between devices: 63.9 us -> none  [the longest x10 50.8 us: extended(): lax.ppermute(tail, axis, [(i, (i + 1) % count) for i in range(ends)])]
    scatter x1 -> x0, local copies, waits for them, and re-layouts: 8.14 us -> none  [per_device(): jnp.zeros((slots_total, bins, channels), jnp.bfloat16).at[slot_index]]
    ppermute x20 -> x0, waiting for transfers between devices: 5.2 us -> none  [the longest x10 5.18 us: extended(): lax.ppermute(tail, axis, [(i, (i + 1) % count) for i in range(ends)])]
    unnamed x24, local copies, waits for them, and re-layouts: 8.81 us -> 13.9 us
    all_to_all x3 -> x2, starting transfers between devices: 27.9 us -> 24.7 us  [the longest x1 17.4 us: per_device(): lax.all_to_all(back.reshape(owners, cap * bins, channels), ('cam', 'tile'...]
    all_to_all x3 -> x2, waiting for transfers between devices: 98.2 us -> 98.1 us  [the longest x1 49.8 us: per_device(): lax.all_to_all(back.reshape(owners, cap * bins, channels), ('cam', 'tile'...]
  transfers between devices with their start and end apart: 23 -> 2, of which waited for: 12 -> 2; matrix products, arithmetic and copies ran while one was open for 6% -> 1% of each run, Pallas kernels for 0% -> 0%
where the time goes in v1:
time: 276 us
  Pallas kernels  126 us (46%)
  waiting for transfers between devices  98.1 us (36%)
  starting transfers between devices  24.7 us (9%)
  local copies, waits for them, and re-layouts  17.4 us (6%)
  other arithmetic  4.79 us (2%)
  matrix products  4.64 us (2%)
    pallas_call x1, Pallas kernels, halo_exchange(): pl.pallas_call(functools.partial(halo_kernel, cams, tiles), out_shape=[ja...  65.6 us
    all_to_all x1, waiting for transfers between devices, per_device(): lax.all_to_all(back.reshape(owners, cap * bins, channels), ('cam', 'tile'...  49.8 us
    all_to_all x1, waiting for transfers between devices, per_device(): lax.all_to_all(sent, ('cam', 'tile'), split_axis=0, concat_axis=0, tiled=...  48.3 us
    pallas_call x1, Pallas kernels, convolve(): pl.pallas_call(functools.partial(conv_kernel, cap, bins, *grid_shape), ou...  47.7 us
    all_to_all x1, starting transfers between devices, per_device(): lax.all_to_all(back.reshape(owners, cap * bins, channels), ('cam', 'tile'...  17.4 us
    unnamed x24, local copies, waits for them, and re-layouts  13.9 us
    pallas_call x1, Pallas kernels, splat(): pl.pallas_call(functools.partial(splat_kernel, cap, bins), out_shape=jax....  10.3 us
    all_to_all x1, starting transfers between devices, per_device(): lax.all_to_all(sent, ('cam', 'tile'), split_axis=0, concat_axis=0, tiled=...  7.3 us
  transfers between devices with their start and end apart: 2, of which 2 were waited for; matrix products, arithmetic and copies ran while one was open for 1% of the time, Pallas kernels for 0%

profile of v1, /device:TPU:0, one launch (start us, length us, event | category | flops | bytes accessed | tf_op | source)
XLA Modules:
  0.0 276.2 jit_solution(3988346462948167600)
XLA Ops:
  0.6 0.5 broadcast.39
  1.1 1.3 multiply_reduce_fusion
  2.5 0.1 reshape.70.owner_ref
  2.6 0.8 reshape.90
  3.4 0.1 pad.5.clone
  3.5 0.8 add_convert_fusion.meta_ref
  4.4 1.6 copy-done.1
  5.9 1.2 copy-done.4
  7.2 2.1 lift.1
  9.3 1.3 copy-done
  10.6 7.3 %all-to-all-start = ((bf16[32,272,128]{2,1,0:T(8,128)(2,1)}), bf16[32,272,128]{2,1,0:T(8,128)(2,1)S(1)}, u32[]{:S(2)}, u32[]{:S(2)}) async-start(bf16[32,272,128]{2,1,0:T(8,128)(2,1)} %copy-done), calls=%async_computation | async-start | bytes 4456448 | tf_op jit(solution)/shard_map/all_to_all | solution.py:423
  17.9 1.8 copy.23
  19.7 0.1 reverse_bitcast_fusion
  19.8 1.1 copy-done.9
  20.9 1.6 pad_maximum_fusion.weight_ref
  22.6 48.3 %all-to-all-done.recv_ref = bf16[32,272,128]{2,1,0:T(8,128)(2,1)S(1)} async-done(((bf16[32,272,128]{2,1,0:T(8,128)(2,1)}), bf16[32,272,128]{2,1,0:T(8,128)(2,1)S(1)}, u32[]{:S(2)}, u32[]{:S(2)}) %all-to-all-start) | async-done | bytes 2228256 | tf_op jit(solution)/shard_map/all_to_all | solution.py:423
  70.9 0.2 convert_reduce_fusion
  71.1 0.1 copy.26
  71.1 0.6 convert_bitcast_fusion.cells_ref
  71.8 10.3 %splat.1.h_ref = bf16[16,256,128]{2,1,0:T(8,128)(2,1)S(1)} custom-call(s32[128]{0:T(128)S(1)} %get-tuple-element.24.tile_ref, s32[128]{0:T(128)S(1)} %get-tuple-element.23.valid_ref, bf16[32,272,128]{2,1,0:T(8,128)(2,1)S(1)} %all-to-all-done.recv_ref), custom_call_target="tpu_custom_call" | custom-call | tf_op jit(solution)/shard_map/splat/pallas_call | solution.py:120
  82.1 1.0 copy-done.3
  83.1 65.6 %halo.1 = (bf16[32,288,128]{2,1,0:T(8,128)(2,1)}, bf16[24,288,128]{2,1,0:T(8,128)(2,1)}) custom-call(bf16[16,256,128]{2,1,0:T(8,128)(2,1)} %copy-done.3, bf16[16,256,128]{2,1,0:T(8,128)(2,1)} %g_ref.1), custom_call_target="tpu_custom_call" | custom-call | tf_op jit(solution)/shard_map/halo/pallas_call | solution.py:224
  148.7 47.7 %convolutions.1 = (bf16[16,256,128]{2,1,0:T(8,128)(2,1)}, bf16[8192,128]{1,0:T(8,128)(2,1)}) custom-call(s32[128]{0:T(128)} %copy-done.7, s32[128]{0:T(128)} %copy-done.6, bf16[32,288,128]{2,1,0:T(8,128)(2,1)} %get-tuple-element.7.hp_ref, bf16[24,288,128]{2,1,0:T(8,128)(2,1)} %get-tuple-element.8.gp_ref, ...), custom_call_target="tpu_custom_call" | custom-call | tf_op jit(solution)/shard_map/convolutions/pallas_call | solution.py:379
  196.3 17.4 %all-to-all-start.1 = ((bf16[32,256,128]{2,1,0:T(8,128)(2,1)}), bf16[32,256,128]{2,1,0:T(8,128)(2,1)S(1)}, u32[]{:S(2)}, u32[]{:S(2)}) async-start(bf16[32,256,128]{2,1,0:T(8,128)(2,1)} %bitcast.33), calls=%async_computation.1 | async-start | bytes 4194304 | tf_op jit(solution)/shard_map/all_to_all | solution.py:436
  213.8 0.1 mul.18
  213.9 0.2 convert_reduce_fusion.2
  214.1 49.8 %all-to-all-done.1 = bf16[32,256,128]{2,1,0:T(8,128)(2,1)S(1)} async-done(((bf16[32,256,128]{2,1,0:T(8,128)(2,1)}), bf16[32,256,128]{2,1,0:T(8,128)(2,1)S(1)}, u32[]{:S(2)}, u32[]{:S(2)}) %all-to-all-start.1) | async-done | bytes 2097184 | tf_op jit(solution)/shard_map/all_to_all | solution.py:436
  263.9 1.3 copy-done.8
  265.2 2.3 gather_fusion
  267.6 2.1 convolution_convert_fusion
  269.7 2.5 convolution_convert_fusion.1
  272.2 3.9 %copy.25 = bf16[4,16,128,128]{3,2,1,0:T(8,128)(2,1)} copy(bf16[4,16,128,128]{2,3,1,0:T(8,128)(2,1)} %bitcast.31) | data formatting | bytes 4194304
  (19 shorter events, 0.1 us)
Async XLA Ops:
  4.3 1.6 copy-start.1
  5.9 1.2 copy-start.4
  9.3 1.3 copy-start
  10.6 60.2 %all-to-all-start = ((bf16[32,272,128]{2,1,0:T(8,128)(2,1)}), bf16[32,272,128]{2,1,0:T(8,128)(2,1)S(1)}, u32[]{:S(2)}, u32[]{:S(2)}) async-start(bf16[32,272,128]{2,1,0:T(8,128)(2,1)} %copy-done), calls=%async_computation | async-start | bytes 4456448 | tf_op jit(solution)/shard_map/all_to_all | solution.py:423
  19.7 1.3 copy-start.9
  71.0 77.6 %copy-start.6 = (s32[128]{0:T(128)}, s32[128]{0:T(128)S(1)}, u32[]{:S(2)}) copy-start(s32[128]{0:T(128)S(1)} %get-tuple-element.23.valid_ref) | copy-start | bytes 1540
  71.0 77.6 %copy-start.7 = (s32[128]{0:T(128)}, s32[128]{0:T(128)S(1)}, u32[]{:S(2)}) copy-start(s32[128]{0:T(128)S(1)} %get-tuple-element.24.tile_ref) | copy-start | bytes 1540
  82.1 1.0 copy-start.3
  196.3 67.5 %all-to-all-start.1 = ((bf16[32,256,128]{2,1,0:T(8,128)(2,1)}), bf16[32,256,128]{2,1,0:T(8,128)(2,1)S(1)}, u32[]{:S(2)}, u32[]{:S(2)}) async-start(bf16[32,256,128]{2,1,0:T(8,128)(2,1)} %bitcast.33), calls=%async_computation.1 | async-start | bytes 4194304 | tf_op jit(solution)/shard_map/all_to_all | solution.py:436
  213.8 53.8 %copy-start.5 = (bf16[4,16,64,128]{3,2,1,0:T(8,128)(2,1)S(1)}, bf16[4,16,64,128]{3,2,1,0:T(8,128)(2,1)}, u32[]{:S(2)}) copy-start(bf16[4,16,64,128]{3,2,1,0:T(8,128)(2,1)} %param.7) | copy-start | bytes 3145732
  263.9 1.3 copy-start.8
  267.6 2.1 copy-start.2

commit v2 on v1

v2 whole, which is shorter than its diff:
```python
import functools

import jax
import jax.numpy as jnp
from jax import lax
from jax.experimental import pallas as pl
from jax.experimental.pallas import tpu as pltpu
from jax.sharding import PartitionSpec as P

TS = 16
LAYERS = 4
ROW_HALO = 2 * LAYERS
COL_HALO = 16
META_ROWS = 16
GROUP = 4
MESH = pl.DeviceIdType.MESH
BF = jnp.bfloat16
F32 = jnp.float32
DIRECTIONS = [(dx, dy) for dx in (-1, 0, 1) for dy in (-1, 0, 1) if (dx, dy) != (0, 0)]


def lift_kernel(cap, bins, owner_ref, meta_ref, depth_ref, context_ref, send_ref, count, meta_rows):
    step = pl.program_id(0)
    owners = send_ref.shape[0]
    blocks = depth_ref.shape[0]

    @pl.when(step == 0)
    def _():
        meta_rows[...] = jnp.zeros_like(meta_rows)

        def clear(o, carry):
            count[o] = 0
            return carry

        lax.fori_loop(0, owners, clear, 0)

    for b in range(blocks):
        owner = owner_ref[step * blocks + b]
        rank = count[owner]
        count[owner] = rank + 1
        lifted = jnp.dot(depth_ref[b], context_ref[b], preferred_element_type=F32).astype(BF)
        send_ref[owner, pl.ds(pl.multiple_of(rank * bins, bins), bins), :] = lifted
        meta_rows[owner, pl.ds(rank, 1), :] = meta_ref[pl.ds(b, 1), :]

    @pl.when(step == pl.num_programs(0) - 1)
    def _():
        def put(o, carry):
            rows = meta_rows[o]
            send_ref[o, cap * bins : cap * bins + META_ROWS, :] = jnp.concatenate(
                [rows, jnp.zeros_like(rows)], axis=0
            ).astype(BF)
            return carry

        lax.fori_loop(0, owners, put, 0)


def lift(depth, context, owner, meta, owners, cap):
    blocks, bins, pixels = depth.shape
    channels = context.shape[2]
    chunk = 16
    rows = cap * bins + META_ROWS
    return pl.pallas_call(
        functools.partial(lift_kernel, cap, bins),
        grid=(blocks // chunk,),
        out_shape=jax.ShapeDtypeStruct((owners, rows, channels), BF),
        in_specs=[
            pl.BlockSpec(memory_space=pltpu.SMEM),
            pl.BlockSpec((chunk, 128), lambda i: (i, 0)),
            pl.BlockSpec((chunk, bins, pixels), lambda i: (i, 0, 0)),
            pl.BlockSpec((chunk, pixels, channels), lambda i: (i, 0, 0)),
        ],
        out_specs=pl.BlockSpec((owners, rows, channels), lambda i: (0, 0, 0)),
        scratch_shapes=[pltpu.SMEM((owners,), jnp.int32), pltpu.VMEM((owners, 8, 128), F32)],
        compiler_params=pltpu.CompilerParams(vmem_limit_bytes=40 << 20),
        name="lift",
    )(owner, meta, depth, context)


def list_slots(valid_ref, chosen):
    def look(slot, count):
        chosen[count] = slot
        return count + valid_ref[slot]

    return lax.fori_loop(0, valid_ref.shape[0], look, 0)


def splat_kernel(cap, bins, tile_ref, valid_ref, meta_ref, recv_ref, out_ref, sums, chosen):
    tiles = sums.shape[0]
    cells = TS * TS
    sums[...] = jnp.zeros_like(sums)
    live_slots = list_slots(valid_ref, chosen)

    def group(step, carry):
        parts = []
        for k in range(GROUP):
            at = step * GROUP + k
            slot = chosen[jnp.minimum(at, live_slots - 1)]
            row = meta_ref[pl.ds(slot, 1), :][:, 0:bins]
            place = jnp.where(at < live_slots, row, -1.0)
            wide = jnp.broadcast_to(place, (cells, bins))
            index = lax.broadcasted_iota(jnp.int32, (cells, bins), 0).astype(F32)
            hot = jnp.where(wide == index, 1.0, 0.0).astype(BF)
            start = pl.multiple_of(slot % cap * bins, bins)
            rows = recv_ref[slot // cap, pl.ds(start, bins), :]
            parts.append((tile_ref[slot], jnp.dot(hot, rows, preferred_element_type=F32)))
        for tile, part in parts:
            sums[tile] = sums[tile] + part
        return carry

    lax.fori_loop(0, (live_slots + GROUP - 1) // GROUP, group, 0)
    for tile in range(tiles):
        for row in range(TS):
            out_ref[row, tile * TS : (tile + 1) * TS, :] = sums[
                tile, row * TS : (row + 1) * TS, :
            ].astype(BF)


def splat(received, slot_tile, slot_valid, slot_meta, cap, bins, rows, cols):
    channels = received.shape[2]
    tiles = (rows // TS) * (cols // TS)
    vmem = pl.BlockSpec(memory_space=pltpu.VMEM)
    smem = pl.BlockSpec(memory_space=pltpu.SMEM)
    return pl.pallas_call(
        functools.partial(splat_kernel, cap, bins),
        out_shape=jax.ShapeDtypeStruct((rows, cols, channels), BF),
        in_specs=[smem, smem, vmem, vmem],
        out_specs=vmem,
        scratch_shapes=[
            pltpu.VMEM((tiles, TS * TS, channels), F32),
            pltpu.SMEM((slot_valid.shape[0] + 1,), jnp.int32),
        ],
        compiler_params=pltpu.CompilerParams(vmem_limit_bytes=40 << 20),
        name="splat",
    )(slot_tile, slot_valid, slot_meta, received)


def halo_kernel(
    cams, tiles, h_ref, g_ref,
    h_ns, h_ew, h_corner, g_ns, g_ew, g_corner,
    h_edge, g_edge, send_sem, recv_sem,
):
    cam = lax.axis_index("cam")
    tile = lax.axis_index("tile")
    rows, cols = h_ref.shape[0], h_ref.shape[1]

    def there(dx, dy):
        ok = None
        for at, step, count in ((cam, dx, cams), (tile, dy, tiles)):
            if step:
                here = (at + step >= 0) & (at + step < count)
                ok = here if ok is None else ok & here
        return ok

    barrier = pltpu.get_barrier_semaphore()
    arrivals = 0
    for dx, dy in DIRECTIONS:
        near = there(dx, dy)
        arrivals = arrivals + near.astype(jnp.int32)

        @pl.when(near)
        def _():
            pl.semaphore_signal(
                barrier, inc=1, device_id=(cam + dx, tile + dy), device_id_type=MESH
            )

    for edge, field in ((h_edge, h_ref), (g_edge, g_ref)):
        edge[0] = field[:, 0:COL_HALO, :]
        edge[1] = field[:, cols - COL_HALO : cols, :]
    pl.semaphore_wait(barrier, arrivals)

    def copies(index):
        dx, dy = DIRECTIONS[index]
        side_row, side_col = (0 if dx == 1 else 1), (0 if dy == 1 else 1)
        own_col = 0 if dy == -1 else 1
        pairs = []
        for field, edge, ns, ew, corner, halo in (
            (h_ref, h_edge, h_ns, h_ew, h_corner, ROW_HALO),
            (g_ref, g_edge, g_ns, g_ew, g_corner, LAYERS),
        ):
            first = 0 if dx == -1 else rows - halo
            if dy == 0:
                for part in range(0, halo, LAYERS):
                    pairs.append(
                        (
                            field.at[pl.ds(first + part, LAYERS)],
                            ns.at[side_row, pl.ds(part, LAYERS)],
                        )
                    )
            elif dx == 0:
                pairs.append((edge.at[own_col], ew.at[side_col]))
            else:
                pairs.append(
                    (edge.at[own_col, pl.ds(first, halo)], corner.at[2 * side_row + side_col])
                )
        return [
            pltpu.make_async_remote_copy(
                src_ref=source,
                dst_ref=target,
                send_sem=send_sem.at[3 * index + which],
                recv_sem=recv_sem.at[3 * index + which],
                device_id=(cam + dx, tile + dy),
                device_id_type=MESH,
            )
            for which, (source, target) in enumerate(pairs)
        ]

    for index in range(len(DIRECTIONS)):
        @pl.when(there(*DIRECTIONS[index]))
        def _():
            for copy in copies(index):
                copy.start()

    for index, (dx, dy) in enumerate(DIRECTIONS):
        @pl.when(there(dx, dy))
        def _():
            for copy in copies(index):
                copy.wait_send()

        @pl.when(there(-dx, -dy))
        def _():
            for copy in copies(index):
                copy.wait_recv()


def halo_exchange(cells, cotangent, cams, tiles):
    rows, cols, channels = cells.shape
    vmem = pl.BlockSpec(memory_space=pltpu.VMEM)

    def parts(halo):
        return [
            jax.ShapeDtypeStruct((2, halo, cols, channels), BF),
            jax.ShapeDtypeStruct((2, rows, COL_HALO, channels), BF),
            jax.ShapeDtypeStruct((4, halo, COL_HALO, channels), BF),
        ]

    return pl.pallas_call(
        functools.partial(halo_kernel, cams, tiles),
        out_shape=parts(ROW_HALO) + parts(LAYERS),
        in_specs=[vmem] * 2,
        out_specs=[vmem] * 6,
        scratch_shapes=[
            pltpu.VMEM((2, rows, COL_HALO, channels), BF),
            pltpu.VMEM((2, rows, COL_HALO, channels), BF),
            pltpu.SemaphoreType.DMA((3 * len(DIRECTIONS),)),
            pltpu.SemaphoreType.DMA((3 * len(DIRECTIONS),)),
        ],
        compiler_params=pltpu.CompilerParams(
            collective_id=0, has_side_effects=True, vmem_limit_bytes=24 << 20
        ),
        name="halo",
    )(cells, cotangent)


def conv_kernel(
    cap, bins, grid_rows, grid_cols,
    tile_ref, valid_ref, h_ref, g_ref, h_ns, h_ew, h_corner, g_ns, g_ew, g_corner,
    weight_ref, cells_ref,
    out_ref, back_ref,
    fields, slopes, masks, wide_weight, grads, outer_grad, chosen,
):
    rows, cols = out_ref.shape[0], out_ref.shape[1]
    channels = out_ref.shape[2]
    width = cols + 2 * COL_HALO
    tall = rows + 2 * ROW_HALO
    row_first = lax.axis_index("cam") * rows - ROW_HALO
    col_first = lax.axis_index("tile") * cols - COL_HALO
    column = lax.broadcasted_iota(jnp.int32, (width, channels), 0) + col_first
    masks[0] = jnp.zeros((width, channels), F32)
    masks[1] = jnp.where((column >= 0) & (column < grid_cols), 1.0, 0.0)
    wide_weight[...] = jnp.zeros_like(wide_weight)

    def mask_of(row):
        at = row + row_first
        return masks[((at >= 0) & (at < grid_rows)).astype(jnp.int32)]

    def put(slot, row, value):
        fields[slot, row, :, 0:channels] = pltpu.roll(value, 1, 0).astype(BF)
        fields[slot, row, :, channels : 2 * channels] = value.astype(BF)
        fields[slot, row, :, 2 * channels : 3 * channels] = pltpu.roll(
            value, width - 1, 0
        ).astype(BF)

    def assemble(field, ns, ew, corner, halo, store):
        def pad(step, left, middle, right):
            row = step + ROW_HALO - halo
            whole = jnp.concatenate([left, middle, right], axis=0).astype(F32)
            store(step, row, jnp.where(mask_of(row) > 0.5, whole, 0.0))

        def upper(i, carry):
            pad(i, corner[0, i], ns[0, i], corner[1, i])
            return carry

        def inner(i, carry):
            pad(i + halo, ew[0, i], field[i], ew[1, i])
            return carry

        def lower(i, carry):
            pad(i + halo + rows, corner[2, i], ns[1, i], corner[3, i])
            return carry

        lax.fori_loop(0, halo, upper, 0)
        lax.fori_loop(0, rows, inner, 0)
        lax.fori_loop(0, halo, lower, 0)

    def keep_grad(step, row, value):
        outer_grad[step] = value.astype(BF)

    assemble(h_ref, h_ns, h_ew, h_corner, ROW_HALO, lambda step, row, value: put(0, row, value))
    assemble(g_ref, g_ns, g_ew, g_corner, LAYERS, keep_grad)

    def spread(index):
        slot = index % 2
        for j in range(2):
            for s in range(3):
                for r in range(3):
                    k = (r + j) * 3 + s
                    wide_weight[
                        slot, k * channels : (k + 1) * channels, j * channels : (j + 1) * channels
                    ] = weight_ref[index, r, s]

    def sweep(index, source, ranges):
        spread(index)
        for first, last, finish in ranges:
            def one(row, finish=finish):
                window = jnp.concatenate([fields[source, row - 1 + k] for k in range(4)], axis=1)
                both = jnp.dot(window, wide_weight[index % 2], preferred_element_type=F32)
                for j in range(2):
                    finish(row + j, both[:, j * channels : (j + 1) * channels])

            def two(step, carry, first=first, one=one):
                one(first + 4 * step)
                one(first + 4 * step + 2)
                return carry

            pairs = (last - first) // 2
            lax.fori_loop(0, pairs // 2, two, 0)
            if pairs % 2:
                one(last - 2)

    def activate(pre):
        sigma = 0.5 * jnp.tanh(0.5 * pre) + 0.5
        value = pre * sigma
        return value, sigma + value * (1.0 - sigma)

    for layer in range(1, LAYERS):
        def finish_forward(row, pre, layer=layer):
            value, slope = activate(pre)
            slopes[layer - 1, row] = slope
            put(layer % 2, row, value * mask_of(row))

        sweep(layer - 1, (layer - 1) % 2, [(layer, tall - layer, finish_forward)])

    def finish_last(row, pre):
        value, slope = activate(pre)
        grad = outer_grad[row - (ROW_HALO - LAYERS)].astype(F32)
        put(LAYERS % 2, row, grad * slope)
        return value

    def finish_own(row, pre):
        value = finish_last(row, pre)
        out_ref[row - ROW_HALO] = value[COL_HALO : COL_HALO + cols].astype(BF)

    sweep(
        LAYERS - 1, (LAYERS - 1) % 2,
        [
            (LAYERS, ROW_HALO, finish_last),
            (ROW_HALO, ROW_HALO + rows, finish_own),
            (ROW_HALO + rows, tall - LAYERS, finish_last),
        ],
    )

    for layer in range(LAYERS, 0, -1):
        done = LAYERS - layer

        def finish_backward(row, grad, layer=layer, done=done):
            grad = grad.astype(BF)
            if layer > 1:
                put(
                    (done + 1) % 2, row,
                    grad.astype(F32) * slopes[layer - 2, row] * mask_of(row),
                )
            else:
                inner = row - ROW_HALO
                for t in range(cols // TS):
                    grads[t, pl.ds(pl.multiple_of(inner * TS, TS), TS), :] = grad[
                        COL_HALO + t * TS : COL_HALO + (t + 1) * TS
                    ]

        sweep(
            LAYERS + layer - 1, done % 2,
            [(ROW_HALO + 1 - layer, ROW_HALO + rows - 1 + layer, finish_backward)],
        )

    slots = cells_ref.shape[1]
    lane = lax.broadcasted_iota(jnp.int32, (bins, slots), 1)
    cell = lax.broadcasted_iota(jnp.int32, (bins, TS * TS), 1).astype(F32)
    live_slots = list_slots(valid_ref, chosen)

    def send_back(step, carry):
        parts = []
        for k in range(GROUP):
            slot = chosen[jnp.minimum(step * GROUP + k, live_slots - 1)]
            place = jnp.sum(jnp.where(lane == slot, cells_ref[...], 0.0), axis=1, keepdims=True)
            hot = jnp.where(place == cell, 1.0, 0.0).astype(BF)
            parts.append(
                (slot, jnp.dot(hot, grads[tile_ref[slot]], preferred_element_type=F32))
            )
        for slot, part in parts:
            back_ref[pl.ds(pl.multiple_of(slot * bins, bins), bins), :] = part.astype(BF)
        return carry

    lax.fori_loop(0, (live_slots + GROUP - 1) // GROUP, send_back, 0)


def convolve(h, g, halos, weights, slot_tile, slot_valid, cells, cap, bins, grid_shape):
    rows, cols, channels = h.shape
    tall, wide = rows + 2 * ROW_HALO, cols + 2 * COL_HALO
    assert rows == TS
    vmem = pl.BlockSpec(memory_space=pltpu.VMEM)
    smem = pl.BlockSpec(memory_space=pltpu.SMEM)
    return pl.pallas_call(
        functools.partial(conv_kernel, cap, bins, *grid_shape),
        out_shape=[
            jax.ShapeDtypeStruct((rows, cols, channels), BF),
            jax.ShapeDtypeStruct((cells.shape[1] * bins, channels), BF),
        ],
        in_specs=[smem, smem] + [vmem] * 10,
        out_specs=[vmem, vmem],
        scratch_shapes=[
            pltpu.VMEM((2, tall, wide, 3 * channels), BF),
            pltpu.VMEM((LAYERS - 1, tall, wide, channels), F32),
            pltpu.VMEM((2, wide, channels), F32),
            pltpu.VMEM((2, 12 * channels, 2 * channels), BF),
            pltpu.VMEM((cols // TS, TS * TS, channels), BF),
            pltpu.VMEM((rows + 2 * LAYERS, wide, channels), BF),
            pltpu.SMEM((slot_valid.shape[0] + 1,), jnp.int32),
        ],
        compiler_params=pltpu.CompilerParams(vmem_limit_bytes=58 << 20),
        name="convolutions",
    )(slot_tile, slot_valid, h, g, *halos, weights, cells)


def final_kernel(slot_ref, depth_ref, context_ref, back_ref, grad_depth_ref, grad_context_ref):
    step = pl.program_id(0)
    blocks = depth_ref.shape[0]
    for b in range(blocks):
        rows = back_ref[slot_ref[step * blocks + b]]
        grad_context_ref[b] = lax.dot_general(
            depth_ref[b], rows, (((0,), (0,)), ((), ())), preferred_element_type=F32
        ).astype(BF)
        grad_depth_ref[b] = lax.dot_general(
            rows, context_ref[b], (((1,), (1,)), ((), ())), preferred_element_type=F32
        ).astype(BF)


def final(slot_index, depth, context, returned):
    blocks, bins, pixels = depth.shape
    channels = context.shape[2]
    chunk = 16
    depth_spec = pl.BlockSpec((chunk, bins, pixels), lambda i: (i, 0, 0))
    context_spec = pl.BlockSpec((chunk, pixels, channels), lambda i: (i, 0, 0))
    return pl.pallas_call(
        final_kernel,
        grid=(blocks // chunk,),
        out_shape=[
            jax.ShapeDtypeStruct(depth.shape, BF),
            jax.ShapeDtypeStruct(context.shape, BF),
        ],
        in_specs=[
            pl.BlockSpec(memory_space=pltpu.SMEM),
            depth_spec,
            context_spec,
            pl.BlockSpec(returned.shape, lambda i: (0, 0, 0)),
        ],
        out_specs=[depth_spec, context_spec],
        compiler_params=pltpu.CompilerParams(vmem_limit_bytes=40 << 20),
        name="final",
    )(slot_index, depth, context, returned)


def per_device(
    depth_weights, context, block_owner, block_local, block_cell, conv_weight, cotangent
):
    cams_here, blocks_cam, bins, pixels = depth_weights.shape
    channels = context.shape[3]
    rows, cols = cotangent.shape[0], cotangent.shape[1]
    cams = lax.axis_size("cam")
    tiles = lax.axis_size("tile")
    owners = cams * tiles
    blocks = cams_here * blocks_cam
    cap = max(2, 2 * blocks // owners)
    depth = depth_weights.reshape(blocks, bins, pixels)
    flat_context = context.reshape(blocks, pixels, channels)
    owner = block_owner.reshape(blocks)
    meta = jnp.concatenate(
        [
            block_cell.reshape(blocks, bins),
            block_local.reshape(blocks, 1),
            jnp.ones((blocks, 1), jnp.int32),
            jnp.zeros((blocks, 128 - bins - 2), jnp.int32),
        ],
        axis=1,
    ).astype(F32)
    sent = lift(depth, flat_context, owner, meta, owners, cap)
    received = lax.all_to_all(sent, ("cam", "tile"), split_axis=0, concat_axis=0, tiled=True)
    slot_meta = received[:, cap * bins : cap * bins + cap, :].reshape(owners * cap, 128)
    slot_tile = slot_meta[:, bins].astype(jnp.int32)
    slot_valid = slot_meta[:, bins + 1].astype(jnp.int32)
    wide_meta = slot_meta.astype(F32)
    slot_cells = wide_meta[:, :bins].T
    backward = jnp.swapaxes(conv_weight[:, ::-1, ::-1], 3, 4)
    weights = jnp.concatenate([conv_weight, backward], axis=0)
    cells = splat(received, slot_tile, slot_valid, wide_meta, cap, bins, rows, cols)
    halos = halo_exchange(cells, cotangent, cams, tiles)
    bev_out, back = convolve(
        cells, cotangent, halos, weights, slot_tile, slot_valid, slot_cells, cap, bins,
        (rows * cams, cols * tiles),
    )
    returned = lax.all_to_all(
        back.reshape(owners, cap * bins, channels),
        ("cam", "tile"), split_axis=0, concat_axis=0, tiled=True,
    ).reshape(owners * cap, bins, channels)
    positions = jnp.arange(blocks, dtype=jnp.int32)
    earlier = (owner[:, None] == owner[None, :]) & (positions[None, :] < positions[:, None])
    slot_index = owner * cap + jnp.sum(earlier.astype(jnp.int32), axis=1)
    grad_depth, grad_context = final(slot_index, depth, flat_context, returned)
    return (
        bev_out,
        grad_depth.reshape(depth_weights.shape),
        grad_context.reshape(context.shape),
    )


def solution(mesh):
    placed = (
        P(("cam", "tile"), None, None, None),
        P(("cam", "tile"), None, None, None),
        P(("cam", "tile"), None, None),
        P(("cam", "tile"), None),
        P(("cam", "tile"), None, None),
        P(),
        P("cam", "tile", None),
    )
    return jax.shard_map(
        per_device,
        mesh=mesh,
        in_specs=placed,
        out_specs=(
            P("cam", "tile", None),
            P(("cam", "tile"), None, None, None),
            P(("cam", "tile"), None, None, None),
        ),
        check_vma=False,
    )
```

time: 276 us -> 209 us (0.76)
  Pallas kernels: 126 us -> 70.2 us
  matrix products: 4.64 us -> 0 us
  local copies, waits for them, and re-layouts: 17.4 us -> 13.9 us
    pallas_call x1 -> x2, Pallas kernels: 65.6 us -> 12.3 us  [the longest x1 7.07 us: halo_exchange(): pl.pallas_call(functools.partial(halo_kernel, cams, tiles), out_shape=par...]
    pallas_call x1, Pallas kernels: 10.3 us -> 5.33 us  [splat(): pl.pallas_call(functools.partial(splat_kernel, cap, bins), out_shape=jax....]
    dot_general x2 -> x0, matrix products: 4.64 us -> none  [the longest x1 2.53 us: per_device(): jnp.einsum('bdc,bpc->bdp', block_grad, flat_context, preferred_element_ty...]
    pallas_call x1, Pallas kernels: 47.7 us -> 50.5 us  [convolve(): pl.pallas_call(functools.partial(conv_kernel, cap, bins, *grid_shape), ou...]
    unnamed x24 -> x34, local copies, waits for them, and re-layouts: 13.9 us -> 11.9 us
  transfers between devices with their start and end apart: 2 -> 2, of which waited for: 2 -> 2; matrix products, arithmetic and copies ran while one was open for 1% -> 2% of each run, Pallas kernels for 0% -> 0%
where the time goes in v2:
time: 209 us; the launch traced here: 210 us
  waiting for transfers between devices  98.2 us (47%)
  Pallas kernels  70.2 us (34%)
  starting transfers between devices  22.2 us (11%)
  local copies, waits for them, and re-layouts  13.9 us (7%)
  other arithmetic  4.18 us (2%)
    pallas_call x1, Pallas kernels, convolve(): pl.pallas_call(functools.partial(conv_kernel, cap, bins, *grid_shape), ou...  50.5 us
    all_to_all x1, waiting for transfers between devices, per_device(): lax.all_to_all(back.reshape(owners, cap * bins, channels), ('cam', 'tile'...  49.9 us
    all_to_all x1, waiting for transfers between devices, per_device(): lax.all_to_all(sent, ('cam', 'tile'), split_axis=0, concat_axis=0, tiled=...  48.3 us
    all_to_all x1, starting transfers between devices, per_device(): lax.all_to_all(back.reshape(owners, cap * bins, channels), ('cam', 'tile'...  14.9 us
    unnamed x34, local copies, waits for them, and re-layouts  11.9 us
    all_to_all x1, starting transfers between devices, per_device(): lax.all_to_all(sent, ('cam', 'tile'), split_axis=0, concat_axis=0, tiled=...  7.3 us
    pallas_call x1, Pallas kernels, halo_exchange(): pl.pallas_call(functools.partial(halo_kernel, cams, tiles), out_shape=par...  7.07 us
    pallas_call x1, Pallas kernels, splat(): pl.pallas_call(functools.partial(splat_kernel, cap, bins), out_shape=jax....  5.33 us
  transfers between devices with their start and end apart: 2, of which 2 were waited for; matrix products, arithmetic and copies ran while one was open for 2% of the time, Pallas kernels for 0%

profile of v2, /device:TPU:0, one launch (start us, length us, event | category | flops | bytes accessed | tf_op | source)
XLA Modules:
  0.0 209.5 jit_solution(11395892803162136841)
XLA Ops:
  0.8 0.5 broadcast.9
  1.3 1.3 reduce.7
  2.6 0.1 reshape.42.owner_ref
  2.7 0.8 reshape.54
  3.5 0.8 add_convert_fusion.meta_ref
  4.4 1.6 copy-done.2
  5.9 1.2 copy-done.5
  7.2 2.1 lift.1
  9.3 1.4 copy-done.1
  10.6 7.3 %all-to-all-start = ((bf16[32,272,128]{2,1,0:T(8,128)(2,1)}), bf16[32,272,128]{2,1,0:T(8,128)(2,1)S(1)}, u32[]{:S(2)}, u32[]{:S(2)}) async-start(bf16[32,272,128]{2,1,0:T(8,128)(2,1)} %copy-done.1), calls=%async_computation | async-start | bytes 4456448 | tf_op jit(solution)/shard_map/all_to_all | solution.py:505
  17.9 1.7 copy.25
  19.6 0.1 reverse_bitcast_fusion
  19.8 1.1 copy-done.15
  20.9 1.6 pad_maximum_fusion.weight_ref
  22.5 48.3 %all-to-all-done.recv_ref = bf16[32,272,128]{2,1,0:T(8,128)(2,1)S(1)} async-done(((bf16[32,272,128]{2,1,0:T(8,128)(2,1)}), bf16[32,272,128]{2,1,0:T(8,128)(2,1)S(1)}, u32[]{:S(2)}, u32[]{:S(2)}) %all-to-all-start) | async-done | bytes 2228256 | tf_op jit(solution)/shard_map/all_to_all | solution.py:505
  70.9 0.2 convert_reduce_fusion
  71.1 0.1 copy.23
  71.2 0.1 copy.24.meta_ref
  71.3 0.6 slice_bitcast_fusion.cells_ref
  71.9 5.3 %splat.1.h_ref = bf16[16,256,128]{2,1,0:T(8,128)(2,1)S(1)} custom-call(s32[128]{0:T(128)S(1)} %get-tuple-element.24.tile_ref, s32[128]{0:T(128)S(1)} %get-tuple-element.23.valid_ref, f32[128,128]{1,0:T(8,128)S(1)} %copy.24.meta_ref, bf16[32,272,128]{2,1,0:T(8,128)(2,1)S(1)} %all-to-all-done.recv_ref), custom_call_target="tpu_custom_call" | custom-call | tf_op jit(solution)/shard_map/splat/pallas_call | solution.py:123
  77.3 7.1 %halo.1 = (bf16[2,8,256,128]{3,2,1,0:T(8,128)(2,1)S(1)}, bf16[2,16,16,128]{3,2,1,0:T(8,128)(2,1)S(1)}, bf16[4,8,16,128]{3,2,1,0:T(8,128)(2,1)S(1)}, bf16[2,4,256...) custom-call(bf16[16,256,128]{2,1,0:T(8,128)(2,1)S(1)} %splat.1.h_ref, ...), custom_call_target="tpu_custom_call" | custom-call | tf_op jit(solution)/shard_map/halo/pallas_call | solution.py:236
  84.4 1.0 copy-done.7
  85.4 0.8 copy-done.8
  86.2 0.6 copy-done.9
  86.9 0.6 copy-done.10
  87.5 0.6 copy-done.11
  88.2 0.6 copy-done.12
  88.8 50.5 %convolutions.1 = (bf16[16,256,128]{2,1,0:T(8,128)(2,1)}, bf16[8192,128]{1,0:T(8,128)(2,1)}) custom-call(s32[128]{0:T(128)} %copy-done.14, s32[128]{0:T(128)} %copy-done.13, bf16[16,256,128]{2,1,0:T(8,128)(2,1)} %copy-done, bf16[16,256,128]{2,1,0:T(8,128)(2,1)} %g_ref.3, bf16[2,8,256,128]{3,2,1,0:T(8,128)(2,1)} %copy-done.7, ...), custom_call_target="tpu_custom_call" | custom-call | tf_op jit(solution)/shard_map/convolutions/pallas_call | solution.py:421
  139.3 14.9 %all-to-all-start.1 = ((bf16[32,256,128]{2,1,0:T(8,128)(2,1)}), bf16[32,256,128]{2,1,0:T(8,128)(2,1)}, u32[]{:S(2)}, u32[]{:S(2)}) async-start(bf16[32,256,128]{2,1,0:T(8,128)(2,1)} %bitcast.18), calls=%async_computation.1 | async-start | bytes 4194304 | tf_op jit(solution)/shard_map/all_to_all | solution.py:519
  154.2 0.2 convert_reduce_fusion.2
  154.4 49.9 %all-to-all-done.1 = bf16[32,256,128]{2,1,0:T(8,128)(2,1)} async-done(((bf16[32,256,128]{2,1,0:T(8,128)(2,1)}), bf16[32,256,128]{2,1,0:T(8,128)(2,1)}, u32[]{:S(2)}, u32[]{:S(2)}) %all-to-all-start.1) | async-done | bytes 2097184 | tf_op jit(solution)/shard_map/all_to_all | solution.py:519
  204.3 5.2 %final.1 = (bf16[64,64,128]{2,1,0:T(8,128)(2,1)}, bf16[64,128,128]{2,1,0:T(8,128)(2,1)}) custom-call(s32[64]{0:T(128)S(1)} %multiply_add_fusion.slot_ref, bf16[64,64,128]{2,1,0:T(8,128)(2,1)S(1)} %bitcast.17, bf16[64,128,128]{2,1,0:T(8,128)(2,1)S(1)} %bitcast.15, bf16[128,64,128]{2,1,0:T(8,128)(2,1)} %bitcast.7.back_ref), custom_call_target="tpu_custom_call" | custom-call | tf_op jit(solution)/shard_map/final/pallas_call | solution.py:462
  (28 shorter events, 0.2 us)
Async XLA Ops:
  4.3 1.6 copy-start.2
  5.9 1.2 copy-start.5
  9.2 1.4 copy-start.1
  10.6 60.2 %all-to-all-start = ((bf16[32,272,128]{2,1,0:T(8,128)(2,1)}), bf16[32,272,128]{2,1,0:T(8,128)(2,1)S(1)}, u32[]{:S(2)}, u32[]{:S(2)}) async-start(bf16[32,272,128]{2,1,0:T(8,128)(2,1)} %copy-done.1), calls=%async_computation | async-start | bytes 4456448 | tf_op jit(solution)/shard_map/all_to_all | solution.py:505
  19.6 1.3 copy-start.15
  22.5 54.8 %copy-start.4 = (bf16[16,256,128]{2,1,0:T(8,128)(2,1)S(1)}, bf16[16,256,128]{2,1,0:T(8,128)(2,1)}, u32[]{:S(2)}) copy-start(bf16[16,256,128]{2,1,0:T(8,128)(2,1)} %g_ref.3) | copy-start | bytes 3145732
  71.1 13.3 %copy-start.13 = (s32[128]{0:T(128)}, s32[128]{0:T(128)S(1)}, u32[]{:S(2)}) copy-start(s32[128]{0:T(128)S(1)} %get-tuple-element.23.valid_ref) | copy-start | bytes 1540
  71.1 13.3 %copy-start.14 = (s32[128]{0:T(128)}, s32[128]{0:T(128)S(1)}, u32[]{:S(2)}) copy-start(s32[128]{0:T(128)S(1)} %get-tuple-element.24.tile_ref) | copy-start | bytes 1540
  77.3 11.5 %copy-start = (bf16[16,256,128]{2,1,0:T(8,128)(2,1)}, bf16[16,256,128]{2,1,0:T(8,128)(2,1)S(1)}, u32[]{:S(2)}) copy-start(bf16[16,256,128]{2,1,0:T(8,128)(2,1)S(1)} %splat.1.h_ref) | copy-start | bytes 3145732
  84.4 1.0 copy-start.7
  85.4 0.8 copy-start.8
  86.2 0.6 copy-start.9
  86.9 0.6 copy-start.10
  87.5 0.7 copy-start.11
  88.2 0.6 copy-start.12
  139.3 65.0 %copy-start.3 = (bf16[4,16,128,128]{3,2,1,0:T(8,128)(2,1)S(1)}, bf16[4,16,128,128]{3,2,1,0:T(8,128)(2,1)}, u32[]{:S(2)}) copy-start(bf16[4,16,128,128]{3,2,1,0:T(8,128)(2,1)} %param.8) | copy-start | bytes 6291460
  139.3 65.0 %copy-start.6 = (bf16[4,16,64,128]{3,2,1,0:T(8,128)(2,1)S(1)}, bf16[4,16,64,128]{3,2,1,0:T(8,128)(2,1)}, u32[]{:S(2)}) copy-start(bf16[4,16,64,128]{3,2,1,0:T(8,128)(2,1)} %param.7) | copy-start | bytes 3145732
  139.3 65.0 %all-to-all-start.1 = ((bf16[32,256,128]{2,1,0:T(8,128)(2,1)}), bf16[32,256,128]{2,1,0:T(8,128)(2,1)}, u32[]{:S(2)}, u32[]{:S(2)}) async-start(bf16[32,256,128]{2,1,0:T(8,128)(2,1)} %bitcast.18), calls=%async_computation.1 | async-start | bytes 4194304 | tf_op jit(solution)/shard_map/all_to_all | solution.py:519

commit v3 on v2

--- a/solution.py
+++ b/solution.py
@@ -253,11 +253,23 @@
 
 def conv_kernel(
     cap, bins, grid_rows, grid_cols,
-    tile_ref, valid_ref, h_ref, g_ref, h_ns, h_ew, h_corner, g_ns, g_ew, g_corner,
-    weight_ref, cells_ref,
+    tile_ref, valid_ref, h_ref, g_ref, h_ns_in, h_ew_in, h_corner_in, g_ns_in, g_ew_in,
+    g_corner_in, weight_ref, cells_ref,
     out_ref, back_ref,
     fields, slopes, masks, wide_weight, grads, outer_grad, chosen,
+    h_ns, h_ew, h_corner, g_ns, g_ew, g_corner, fetch_sem,
 ):
+    fetches = [
+        pltpu.make_async_copy(source, target, fetch_sem.at[which])
+        for which, (source, target) in enumerate(
+            (
+                (h_ns_in, h_ns), (h_ew_in, h_ew), (h_corner_in, h_corner),
+                (g_ns_in, g_ns), (g_ew_in, g_ew), (g_corner_in, g_corner),
+            )
+        )
+    ]
+    for fetch in fetches:
+        fetch.start()
     rows, cols = out_ref.shape[0], out_ref.shape[1]
     channels = out_ref.shape[2]
     width = cols + 2 * COL_HALO
@@ -302,6 +314,9 @@
         lax.fori_loop(0, rows, inner, 0)
         lax.fori_loop(0, halo, lower, 0)
 
+    for fetch in fetches:
+        fetch.wait()
+
     def keep_grad(step, row, value):
         outer_grad[step] = value.astype(BF)
 
@@ -321,21 +336,36 @@
     def sweep(index, source, ranges):
         spread(index)
         for first, last, finish in ranges:
-            def one(row, finish=finish):
-                window = jnp.concatenate([fields[source, row - 1 + k] for k in range(4)], axis=1)
+            def some(row, count, finish=finish):
+                window = jnp.concatenate(
+                    [
+                        jnp.concatenate(
+                            [fields[source, row - 1 + k + 2 * pair] for pair in range(count)],
+                            axis=0,
+                        )
+                        for k in range(4)
+                    ],
+                    axis=1,
+                )
                 both = jnp.dot(window, wide_weight[index % 2], preferred_element_type=F32)
-                for j in range(2):
-                    finish(row + j, both[:, j * channels : (j + 1) * channels])
-
-            def two(step, carry, first=first, one=one):
-                one(first + 4 * step)
-                one(first + 4 * step + 2)
+                for pair in range(count):
+                    for j in range(2):
+                        finish(
+                            row + 2 * pair + j,
+                            both[
+                                pair * width : (pair + 1) * width,
+                                j * channels : (j + 1) * channels,
+                            ],
+                        )
+
+            def step_of(step, carry, first=first, some=some):
+                some(first + 4 * step, 2)
                 return carry
 
             pairs = (last - first) // 2
-            lax.fori_loop(0, pairs // 2, two, 0)
+            lax.fori_loop(0, pairs // 2, step_of, 0)
             if pairs % 2:
-                one(last - 2)
+                some(last - 2, 1)
 
     def activate(pre):
         sigma = 0.5 * jnp.tanh(0.5 * pre) + 0.5
@@ -424,7 +454,7 @@
             jax.ShapeDtypeStruct((rows, cols, channels), BF),
             jax.ShapeDtypeStruct((cells.shape[1] * bins, channels), BF),
         ],
-        in_specs=[smem, smem] + [vmem] * 10,
+        in_specs=[smem, smem, vmem, vmem] + [pl.BlockSpec(memory_space=pl.ANY)] * 6 + [vmem] * 2,
         out_specs=[vmem, vmem],
         scratch_shapes=[
             pltpu.VMEM((2, tall, wide, 3 * channels), BF),
@@ -434,7 +464,9 @@
             pltpu.VMEM((cols // TS, TS * TS, channels), BF),
             pltpu.VMEM((rows + 2 * LAYERS, wide, channels), BF),
             pltpu.SMEM((slot_valid.shape[0] + 1,), jnp.int32),
-        ],
+        ]
+        + [pltpu.VMEM(part.shape, BF) for part in halos]
+        + [pltpu.SemaphoreType.DMA((len(halos),))],
         compiler_params=pltpu.CompilerParams(vmem_limit_bytes=58 << 20),
         name="convolutions",
     )(slot_tile, slot_valid, h, g, *halos, weights, cells)

time: 209 us -> 208 us (level); the launches traced: 210 us -> 206 us
  starting transfers between devices: 22.2 us -> 16.9 us
    all_to_all x1, starting transfers between devices: 14.9 us -> 9.6 us  [per_device(): lax.all_to_all(back.reshape(owners, cap * bins, channels), ('cam', 'tile'...]
    pallas_call x1, Pallas kernels: 7.07 us -> 9.66 us  [halo_exchange(): pl.pallas_call(functools.partial(halo_kernel, cams, tiles), out_shape=par...]
where the time goes in v3:
time: 208 us; the launch traced here: 206 us
  waiting for transfers between devices  98.2 us (47%)
  Pallas kernels  71.8 us (35%)
  starting transfers between devices  16.9 us (8%)
  local copies, waits for them, and re-layouts  13.9 us (7%)
  other arithmetic  4.18 us (2%)
    all_to_all x1, waiting for transfers between devices, per_device(): lax.all_to_all(back.reshape(owners, cap * bins, channels), ('cam', 'tile'...  49.9 us
    pallas_call x1, Pallas kernels, convolve(): pl.pallas_call(functools.partial(conv_kernel, cap, bins, *grid_shape), ou...  49.3 us
    all_to_all x1, waiting for transfers between devices, per_device(): lax.all_to_all(sent, ('cam', 'tile'), split_axis=0, concat_axis=0, tiled=...  48.3 us
    unnamed x34, local copies, waits for them, and re-layouts  11.9 us
    pallas_call x1, Pallas kernels, halo_exchange(): pl.pallas_call(functools.partial(halo_kernel, cams, tiles), out_shape=par...  9.66 us
    all_to_all x1, starting transfers between devices, per_device(): lax.all_to_all(back.reshape(owners, cap * bins, channels), ('cam', 'tile'...  9.6 us
    all_to_all x1, starting transfers between devices, per_device(): lax.all_to_all(sent, ('cam', 'tile'), split_axis=0, concat_axis=0, tiled=...  7.3 us
    pallas_call x1, Pallas kernels, splat(): pl.pallas_call(functools.partial(splat_kernel, cap, bins), out_shape=jax....  5.57 us
  transfers between devices with their start and end apart: 2, of which 2 were waited for; matrix products, arithmetic and copies ran while one was open for 2% of the time, Pallas kernels for 0%

profile of v3, /device:TPU:0, one launch (start us, length us, event | category | flops | bytes accessed | tf_op | source)
XLA Modules:
  0.0 205.9 jit_solution(17332038720950032649)
XLA Ops:
  0.8 0.5 broadcast.9
  1.3 1.3 reduce.7
  2.6 0.1 reshape.42.owner_ref
  2.7 0.8 reshape.54
  3.5 0.8 add_convert_fusion.meta_ref
  4.4 1.6 copy-done.2
  5.9 1.2 copy-done.5
  7.2 2.1 %lift.1 = bf16[32,272,128]{2,1,0:T(8,128)(2,1)S(1)} custom-call(s32[64]{0:T(128)S(1)} %reshape.42.owner_ref, f32[64,128]{1,0:T(8,128)S(1)} %add_convert_fusion.meta_ref, bf16[64,64,128]{2,1,0:T(8,128)(2,1)S(1)} %bitcast.16, bf16[64,128,128]{2,1,0:T(8,128)(2,1)S(1)} %bitcast.14), custom_call_target="tpu_custom_call" | custom-call | tf_op jit(solution)/shard_map/lift/pallas_call | solution.py:62
  9.3 1.4 copy-done.1
  10.6 7.3 %all-to-all-start = ((bf16[32,272,128]{2,1,0:T(8,128)(2,1)}), bf16[32,272,128]{2,1,0:T(8,128)(2,1)S(1)}, u32[]{:S(2)}, u32[]{:S(2)}) async-start(bf16[32,272,128]{2,1,0:T(8,128)(2,1)} %copy-done.1), calls=%async_computation | async-start | bytes 4456448 | tf_op jit(solution)/shard_map/all_to_all | solution.py:537
  17.9 1.7 copy.25
  19.6 0.1 reverse_bitcast_fusion
  19.8 1.1 copy-done.15
  20.9 1.6 pad_maximum_fusion.weight_ref
  22.5 48.3 %all-to-all-done.recv_ref = bf16[32,272,128]{2,1,0:T(8,128)(2,1)S(1)} async-done(((bf16[32,272,128]{2,1,0:T(8,128)(2,1)}), bf16[32,272,128]{2,1,0:T(8,128)(2,1)S(1)}, u32[]{:S(2)}, u32[]{:S(2)}) %all-to-all-start) | async-done | bytes 2228256 | tf_op jit(solution)/shard_map/all_to_all | solution.py:537
  70.9 0.2 convert_reduce_fusion
  71.1 0.1 copy.23
  71.2 0.1 copy.24.meta_ref
  71.3 0.6 slice_bitcast_fusion.cells_ref
  71.9 5.6 %splat.1.h_ref = bf16[16,256,128]{2,1,0:T(8,128)(2,1)S(1)} custom-call(s32[128]{0:T(128)S(1)} %get-tuple-element.24.tile_ref, s32[128]{0:T(128)S(1)} %get-tuple-element.23.valid_ref, f32[128,128]{1,0:T(8,128)S(1)} %copy.24.meta_ref, bf16[32,272,128]{2,1,0:T(8,128)(2,1)S(1)} %all-to-all-done.recv_ref), custom_call_target="tpu_custom_call" | custom-call | tf_op jit(solution)/shard_map/splat/pallas_call | solution.py:123
  77.5 9.7 %halo.1 = (bf16[2,8,256,128]{3,2,1,0:T(8,128)(2,1)S(1)}, bf16[2,16,16,128]{3,2,1,0:T(8,128)(2,1)S(1)}, bf16[4,8,16,128]{3,2,1,0:T(8,128)(2,1)S(1)}, bf16[2,4,256...) custom-call(bf16[16,256,128]{2,1,0:T(8,128)(2,1)S(1)} %splat.1.h_ref, ...), custom_call_target="tpu_custom_call" | custom-call | tf_op jit(solution)/shard_map/halo/pallas_call | solution.py:236
  87.2 1.0 copy-done.7
  88.2 0.8 copy-done.8
  89.0 0.6 copy-done.9
  89.7 0.6 copy-done.10
  90.3 0.6 copy-done.11
  91.0 0.6 copy-done.12
  91.6 49.3 %convolutions.1 = (bf16[16,256,128]{2,1,0:T(8,128)(2,1)}, bf16[8192,128]{1,0:T(8,128)(2,1)}) custom-call(s32[128]{0:T(128)} %copy-done.14, s32[128]{0:T(128)} %copy-done.13, bf16[16,256,128]{2,1,0:T(8,128)(2,1)} %copy-done, bf16[16,256,128]{2,1,0:T(8,128)(2,1)} %g_ref.3, bf16[2,8,256,128]{3,2,1,0:T(8,128)(2,1)} %copy-done.7, ...), custom_call_target="tpu_custom_call" | custom-call | tf_op jit(solution)/shard_map/convolutions/pallas_call | solution.py:451
  141.0 9.6 %all-to-all-start.1 = ((bf16[32,256,128]{2,1,0:T(8,128)(2,1)}), bf16[32,256,128]{2,1,0:T(8,128)(2,1)}, u32[]{:S(2)}, u32[]{:S(2)}) async-start(bf16[32,256,128]{2,1,0:T(8,128)(2,1)} %bitcast.18), calls=%async_computation.1 | async-start | bytes 4194304 | tf_op jit(solution)/shard_map/all_to_all | solution.py:551
  150.6 0.2 convert_reduce_fusion.2
  150.8 49.9 %all-to-all-done.1 = bf16[32,256,128]{2,1,0:T(8,128)(2,1)} async-done(((bf16[32,256,128]{2,1,0:T(8,128)(2,1)}), bf16[32,256,128]{2,1,0:T(8,128)(2,1)}, u32[]{:S(2)}, u32[]{:S(2)}) %all-to-all-start.1) | async-done | bytes 2097184 | tf_op jit(solution)/shard_map/all_to_all | solution.py:551
  200.6 5.2 %final.1 = (bf16[64,64,128]{2,1,0:T(8,128)(2,1)}, bf16[64,128,128]{2,1,0:T(8,128)(2,1)}) custom-call(s32[64]{0:T(128)S(1)} %multiply_add_fusion.slot_ref, bf16[64,64,128]{2,1,0:T(8,128)(2,1)S(1)} %bitcast.17, bf16[64,128,128]{2,1,0:T(8,128)(2,1)S(1)} %bitcast.15, bf16[128,64,128]{2,1,0:T(8,128)(2,1)} %bitcast.7.back_ref), custom_call_target="tpu_custom_call" | custom-call | tf_op jit(solution)/shard_map/final/pallas_call | solution.py:494
  (28 shorter events, 0.2 us)
Async XLA Ops:
  4.3 1.6 copy-start.2
  5.9 1.2 copy-start.5
  9.2 1.4 copy-start.1
  10.6 60.2 %all-to-all-start = ((bf16[32,272,128]{2,1,0:T(8,128)(2,1)}), bf16[32,272,128]{2,1,0:T(8,128)(2,1)S(1)}, u32[]{:S(2)}, u32[]{:S(2)}) async-start(bf16[32,272,128]{2,1,0:T(8,128)(2,1)} %copy-done.1), calls=%async_computation | async-start | bytes 4456448 | tf_op jit(solution)/shard_map/all_to_all | solution.py:537
  19.6 1.3 copy-start.15
  22.5 55.0 %copy-start.4 = (bf16[16,256,128]{2,1,0:T(8,128)(2,1)S(1)}, bf16[16,256,128]{2,1,0:T(8,128)(2,1)}, u32[]{:S(2)}) copy-start(bf16[16,256,128]{2,1,0:T(8,128)(2,1)} %g_ref.3) | copy-start | bytes 3145732
  71.1 16.2 %copy-start.13 = (s32[128]{0:T(128)}, s32[128]{0:T(128)S(1)}, u32[]{:S(2)}) copy-start(s32[128]{0:T(128)S(1)} %get-tuple-element.23.valid_ref) | copy-start | bytes 1540
  71.1 16.2 %copy-start.14 = (s32[128]{0:T(128)}, s32[128]{0:T(128)S(1)}, u32[]{:S(2)}) copy-start(s32[128]{0:T(128)S(1)} %get-tuple-element.24.tile_ref) | copy-start | bytes 1540
  77.5 14.1 %copy-start = (bf16[16,256,128]{2,1,0:T(8,128)(2,1)}, bf16[16,256,128]{2,1,0:T(8,128)(2,1)S(1)}, u32[]{:S(2)}) copy-start(bf16[16,256,128]{2,1,0:T(8,128)(2,1)S(1)} %splat.1.h_ref) | copy-start | bytes 3145732
  87.2 1.0 copy-start.7
  88.2 0.8 copy-start.8
  89.0 0.6 copy-start.9
  89.7 0.6 copy-start.10
  90.3 0.7 copy-start.11
  91.0 0.6 copy-start.12
  140.9 59.7 %copy-start.3 = (bf16[4,16,128,128]{3,2,1,0:T(8,128)(2,1)S(1)}, bf16[4,16,128,128]{3,2,1,0:T(8,128)(2,1)}, u32[]{:S(2)}) copy-start(bf16[4,16,128,128]{3,2,1,0:T(8,128)(2,1)} %param.8) | copy-start | bytes 6291460
  140.9 59.7 %copy-start.6 = (bf16[4,16,64,128]{3,2,1,0:T(8,128)(2,1)S(1)}, bf16[4,16,64,128]{3,2,1,0:T(8,128)(2,1)}, u32[]{:S(2)}) copy-start(bf16[4,16,64,128]{3,2,1,0:T(8,128)(2,1)} %param.7) | copy-start | bytes 3145732
  141.0 59.7 %all-to-all-start.1 = ((bf16[32,256,128]{2,1,0:T(8,128)(2,1)}), bf16[32,256,128]{2,1,0:T(8,128)(2,1)}, u32[]{:S(2)}, u32[]{:S(2)}) async-start(bf16[32,256,128]{2,1,0:T(8,128)(2,1)} %bitcast.18), calls=%async_computation.1 | async-start | bytes 4194304 | tf_op jit(solution)/shard_map/all_to_all | solution.py:551
